TPU v7x, 32 devices: a whole 2x2x4 slice. The times are simulated.
32 devices in a mesh: group: 2 (over x), node: 8 (over z, y), head: 2 (over core).
Axes of the slice: x: 2, y: 2, z: 4, core: 2. Of those that a mesh axis runs over, the one named last changes fastest.
Arguments:
- queries_one: bfloat16 [16, 128, 64, 128], P(('group', 'node'), None, 'head'), parts along dimension 0, may hold values from -80 to 80
- keys_one: bfloat16 [16, 128, 8, 128], P(('group', 'node'), None, 'head'), parts along dimension 0, may hold values from -8 to 8
- values_one: bfloat16 [16, 128, 8, 128], P(('group', 'node'), None, 'head'), parts along dimension 0, may hold values from -6 to 6
- queries_two: bfloat16 [16, 128, 64, 128], P(('group', 'node'), None, 'head'), parts along dimension 0, may hold values from -80 to 80
- keys_two: bfloat16 [16, 128, 8, 128], P(('group', 'node'), None, 'head'), parts along dimension 0, may hold values from -8 to 8
- values_two: bfloat16 [16, 128, 8, 128], P(('group', 'node'), None, 'head'), parts along dimension 0, may hold values from -6 to 6
- cache_keys: bfloat16 [512, 128, 8, 128], P(('group', 'node'), None, 'head'), parts along dimension 0, may hold values from -8 to 8
- cache_values: bfloat16 [512, 128, 8, 128], P(('group', 'node'), None, 'head'), parts along dimension 0, may hold values from -6 to 6
- paths: int32 [16, 32], P('group'), parts along dimension 0, may hold values from 0 to 255, as said below
- parents: int32 [16], P('group'), parts along dimension 0, may hold values from 0 to 7
- positions: int32 [2, 16, 128], P(None, ('group', 'node')), parts along dimension 1, may hold values from 0 to 8446, as said below
Outputs:
- attended_one: bfloat16 [16, 128, 64, 128], P(('group', 'node'), None, 'head'), parts along dimension 0
- attended_two: bfloat16 [16, 128, 64, 128], P(('group', 'node'), None, 'head'), parts along dimension 0
There are 2 independent parts, one for each index of `group`. A program takes and returns all parts, laid end to end along the dimension named above; each array names one. Nothing has to cross between parts.
Inputs may be any that keep to these rules, and one draw needn't show every extreme that they name: Each row paths[c] names 32 different cache blocks. Block b lies on device b // 32 of node, and each row names exactly 4 blocks of every device of node. positions[d, c, t] = s + (32 + d) * 128 + t, with one offset s of 0 to 4095 for a tree.
All inputs are finite; a program needn't handle non-finite values.
Results may differ from a plain program's by a relative error of at most 0.012.
The roundings to bfloat16 on the way count: a program that leaves them out, or rounds other values in their place, can miss the bound.
Values may be sent and summed in bfloat16 or wider, within the bound.
No kernel may reach another device: no remote copies, remote signals or barrier semaphores. Data moves between devices by JAX's collectives and lax.ppermute only.
A program may use at most 128 MiB of HBM per device.

v0:
```python
import jax
import jax.numpy as jnp
from jax import lax
from jax.sharding import PartitionSpec as P

rope_theta = 500000.0


def rotary(vector, position_row):
    head_width = vector.shape[-1]
    half_width = head_width // 2
    frequency = rope_theta ** (-(jnp.arange(half_width, dtype=jnp.float32) * 2.0) / head_width)
    angles = position_row.astype(jnp.float32)[:, None] * frequency[None, :]
    cosine = jnp.cos(angles)[:, None, :]
    sine_part = jnp.sin(angles)[:, None, :]
    widened = vector.astype(jnp.float32)
    first_half = widened[..., :half_width]
    second_half = widened[..., half_width:]
    turned = jnp.concatenate(
        [
            first_half * cosine - second_half * sine_part,
            second_half * cosine + first_half * sine_part,
        ],
        -1,
    )
    return turned.astype(jnp.bfloat16)


def attend(query, key_rows, value_rows, score_scale):
    row_count, head_count, head_width = query.shape
    key_count = key_rows.shape[0]
    kv_count = key_rows.shape[1]
    group_size = head_count // kv_count
    grouped = jnp.moveaxis(query.reshape(row_count, kv_count, group_size, head_width), 0, 2)
    key_heads = jnp.moveaxis(key_rows, 1, 0)
    value_heads = jnp.moveaxis(value_rows, 1, 0)
    token_index = lax.broadcasted_iota(jnp.int32, (row_count, key_count), 0)
    key_index = lax.broadcasted_iota(jnp.int32, (row_count, key_count), 1)
    visible = key_index - (key_count - row_count) <= token_index

    def one_head(operands):
        query_head, key_head, value_head = operands
        scores = (
            jnp.einsum("gtd,sd->gts", query_head, key_head, preferred_element_type=jnp.float32)
            * score_scale
        )
        scores = jnp.where(visible[None], scores, -1e30)
        row_max = jnp.max(scores, axis=-1, keepdims=True)
        weights = jnp.exp(scores - row_max)
        total_weight = jnp.sum(weights, axis=-1, keepdims=True)
        mixture = jnp.einsum(
            "gts,sd->gtd",
            weights.astype(jnp.bfloat16),
            value_head,
            preferred_element_type=jnp.float32,
        )
        return (mixture / total_weight).astype(jnp.bfloat16)

    result = lax.map(one_head, (grouped, key_heads, value_heads))
    return jnp.moveaxis(result, 2, 0).reshape(row_count, head_count, head_width)


def outgoing(path_table, cache_keys, cache_values, here_index, per_peer):
    per_owner = cache_keys.shape[0]
    is_local = path_table // per_owner == here_index
    local_block = path_table % per_owner
    slot_rank = jnp.cumsum(is_local.astype(jnp.int32), axis=1) - 1
    slot_range = jnp.arange(per_peer, dtype=jnp.int32)
    selected = jnp.logical_and(
        is_local[:, :, None], slot_rank[:, :, None] == slot_range[None, None, :]
    )
    block_index = jnp.sum(jnp.where(selected, local_block[:, :, None], 0), axis=1)
    return (cache_keys[block_index], cache_values[block_index])


def local(
    queries_one,
    keys_one,
    values_one,
    queries_two,
    keys_two,
    values_two,
    cache_keys,
    cache_values,
    paths,
    parents,
    positions,
):
    here_index = lax.axis_index("node")
    peer_count = lax.axis_size("node")
    per_peer = cache_keys.shape[0] // peer_count
    kv_count = cache_keys.shape[2]
    head_width = cache_keys.shape[3]
    score_scale = head_width ** (-0.5)
    query_rot_one = rotary(queries_one[0], positions[0, 0])
    key_rot_one = rotary(keys_one[0], positions[0, 0])
    query_rot_two = rotary(queries_two[0], positions[1, 0])
    key_rot_two = rotary(keys_two[0], positions[1, 0])
    span_ids = jnp.arange(paths.shape[0], dtype=jnp.int32)
    parent_onehot = (parents[:, None] == span_ids[None, :]).astype(jnp.int32)
    paths_two = jnp.sum(parent_onehot[:, :, None] * paths[None, :, :], axis=1)
    send_keys_one, send_values_one = outgoing(paths, cache_keys, cache_values, here_index, per_peer)
    send_keys_two, send_values_two = outgoing(
        paths_two, cache_keys, cache_values, here_index, per_peer
    )
    is_parent = (parents == here_index)[:, None, None, None, None]
    extra_keys = jnp.where(
        is_parent, key_rot_one[None, None], jnp.zeros_like(key_rot_one)[None, None]
    )
    extra_values = jnp.where(
        is_parent, values_one[0][None, None], jnp.zeros_like(values_one[0])[None, None]
    )
    send_keys_two = jnp.concatenate([send_keys_two, extra_keys], 1)
    send_values_two = jnp.concatenate([send_values_two, extra_values], 1)
    fetched_keys_one, fetched_values_one = (
        lax.all_to_all(send_keys_one, "node", split_axis=0, concat_axis=0, tiled=True),
        lax.all_to_all(send_values_one, "node", split_axis=0, concat_axis=0, tiled=True),
    )
    key_rows = jnp.concatenate([fetched_keys_one.reshape(-1, kv_count, head_width), key_rot_one], 0)
    value_rows = jnp.concatenate(
        [fetched_values_one.reshape(-1, kv_count, head_width), values_one[0]], 0
    )
    attended_one = attend(query_rot_one, key_rows, value_rows, score_scale)
    fetched_keys_two, fetched_values_two = (
        lax.all_to_all(send_keys_two, "node", split_axis=0, concat_axis=0, tiled=True),
        lax.all_to_all(send_values_two, "node", split_axis=0, concat_axis=0, tiled=True),
    )
    parent_keys = jnp.sum(fetched_keys_two[:, per_peer].astype(jnp.float32), axis=0).astype(
        jnp.bfloat16
    )
    parent_values = jnp.sum(fetched_values_two[:, per_peer].astype(jnp.float32), axis=0).astype(
        jnp.bfloat16
    )
    ancestor_keys = fetched_keys_two[:, :per_peer].reshape(-1, kv_count, head_width)
    ancestor_values = fetched_values_two[:, :per_peer].reshape(-1, kv_count, head_width)
    key_rows_two = jnp.concatenate([ancestor_keys, parent_keys, key_rot_two], 0)
    value_rows_two = jnp.concatenate([ancestor_values, parent_values, values_two[0]], 0)
    attended_two = attend(query_rot_two, key_rows_two, value_rows_two, score_scale)
    return (attended_one[None], attended_two[None])


def solution(mesh):
    in_specs = (
        P(("group", "node"), None, "head", None),
        P(("group", "node"), None, "head", None),
        P(("group", "node"), None, "head", None),
        P(("group", "node"), None, "head", None),
        P(("group", "node"), None, "head", None),
        P(("group", "node"), None, "head", None),
        P(("group", "node"), None, "head", None),
        P(("group", "node"), None, "head", None),
        P("group", None),
        P("group"),
        P(None, ("group", "node"), None),
    )
    out_specs = (P(("group", "node"), None, "head", None), P(("group", "node"), None, "head", None))
    return jax.shard_map(local, mesh=mesh, in_specs=in_specs, out_specs=out_specs, check_vma=False)
```

profile of v0, /device:TPU:0, one launch (start us, length us, event | category | flops | bytes accessed | tf_op | source)
XLA Modules:
  0.0 591.4 jit_solution(6580554296833747113)
XLA Ops:
  4.1 7.9 %gather_fusion = bf16[32,128,4,128]{3,2,1,0:T(4,128)(2,1)} fusion(bf16[32,128,4,128]{3,2,1,0:T(4,128)(2,1)} %param.21, s32[1024]{0:T(1024)S(1)} %pad_clamp_fusion.1), kind=kCustom, calls=%fused_computation | custom fusion | bytes 8388736 | tf_op jit(solution)/shard_map/gather | solution.py:73
  12.0 5.4 copy.105
  17.4 7.3 %all-to-all-start = ((bf16[8,4,128,4,128]{4,2,1,3,0:T(8,128)(2,1)}), bf16[8,4,128,4,128]{4,2,1,3,0:T(8,128)(2,1)}, u32[]{:S(2)}, u32[]{:S(2)}) async-start(bf16[8,4,128,4,128]{4,2,1,3,0:T(8,128)(2,1)} %copy.105), calls=%async_computation | async-start | bytes 8388608 | tf_op jit(solution)/shard_map/all_to_all | solution.py:116
  24.7 7.9 %gather_fusion.1 = bf16[32,128,4,128]{3,2,1,0:T(4,128)(2,1)} fusion(bf16[32,128,4,128]{3,2,1,0:T(4,128)(2,1)} %param.22, s32[1024]{0:T(1024)S(1)} %pad_clamp_fusion.1), kind=kCustom, calls=%fused_computation.1 | custom fusion | bytes 8388736 | tf_op jit(solution)/shard_map/gather | solution.py:73
  32.6 5.2 copy.109
  37.8 80.1 %all-to-all-done = bf16[8,4,128,4,128]{4,2,1,3,0:T(8,128)(2,1)} async-done(((bf16[8,4,128,4,128]{4,2,1,3,0:T(8,128)(2,1)}), bf16[8,4,128,4,128]{4,2,1,3,0:T(8,128)(2,1)}, u32[]{:S(2)}, u32[]{:S(2)}) %all-to-all-start) | async-done | bytes 4194336 | tf_op jit(solution)/shard_map/all_to_all | solution.py:116
  117.9 4.5 all-to-all-start.1
  123.1 7.9 %gather_fusion.2 = bf16[32,128,4,128]{3,2,1,0:T(4,128)(2,1)} fusion(bf16[32,128,4,128]{3,2,1,0:T(4,128)(2,1)} %param.21, s32[1024]{0:T(1024)S(1)} %pad_clamp_fusion), kind=kCustom, calls=%fused_computation.2 | custom fusion | bytes 8388736 | tf_op jit(solution)/shard_map/gather | solution.py:73
  131.0 3.4 copy.116
  136.0 3.4 copy.117
  139.4 75.7 %all-to-all-done.1 = bf16[8,4,128,4,128]{4,2,1,3,0:T(8,128)(2,1)} async-done(((bf16[8,4,128,4,128]{4,2,1,3,0:T(8,128)(2,1)}), bf16[8,4,128,4,128]{4,2,1,3,0:T(8,128)(2,1)}, u32[]{:S(2)}, u32[]{:S(2)}) %all-to-all-start.1) | async-done | bytes 4194336 | tf_op jit(solution)/shard_map/all_to_all | solution.py:117
  215.1 4.8 all-to-all-start.2
  219.9 8.1 %gather_fusion.3 = bf16[32,128,4,128]{3,2,1,0:T(4,128)(2,1)} fusion(bf16[32,128,4,128]{3,2,1,0:T(4,128)(2,1)} %param.22, s32[1024]{0:T(1024)S(1)} %pad_clamp_fusion), kind=kCustom, calls=%fused_computation.3 | custom fusion | bytes 8388736 | tf_op jit(solution)/shard_map/gather | solution.py:73
  235.7 3.5 copy.121
  242.7 2.5 copy.106
  245.2 2.5 copy.110
  247.7 2.8 maximum_bitcast_fusion.2
  252.8 82.0 %all-to-all-done.2 = bf16[8,5,128,4,128]{4,2,1,3,0:T(8,128)(2,1)} async-done(((bf16[8,5,128,4,128]{4,2,1,3,0:T(8,128)(2,1)}), bf16[8,5,128,4,128]{4,2,1,3,0:T(8,128)(2,1)}, u32[]{:S(2)}, u32[]{:S(2)}) %all-to-all-start.2) | async-done | bytes 5242912 | tf_op jit(solution)/shard_map/all_to_all | solution.py:125
  334.8 4.9 all-to-all-start.3
  339.9 110.8 %while.22 = (s32[]{:T(128)}, bf16[4,8,128,128]{3,2,1,0:T(8,128)(2,1)S(1)}, bf16[4,8,128,128]{3,2,1,0:T(8,128)(2,1)S(1)}, bf16[4,4224,128]{2,1,0:T(8,128)(2,1)}, ...) while((s32[]{:T(128)}, bf16[4,8,128,128]{3,2,1,0:T(8,128)(2,1)S(1)}, ...), condition=%wide.region_5.6_spmd.clone, body=%wide.region_2.5_spmd.clone.sunk | while | flops 2262972416 | bytes 56793684 | solution.py:59
  340.2 9.0 %fusion.103 = (f32[8,128]{1,0:T(8,128)S(1)}, f32[8,128,4224]{2,1,0:T(8,128)}) fusion(pred[128,4224]{1,0:T(8,128)(4,1)S(1)} %iota_compare_fusion.7, bf16[4,4224,128]{2,1,0:T(8,128)(2,1)} %get-tuple-element.251, s32[]{:T(128)S(6)} %copy.145, bf16[4,8,128,128]{3,2,1,0:T(8,128)(2,1)S(1)} %get-tuple-element.250), kind=kOutput, calls=%fused_computation.8.clone.1 | convolution fusion | flops 1120271360 | bytes 19190784 | tf_op jit(solution)/shard_map/while/body/eval_jaxpr/gtd,sd->gts/dot_general | solution.py:44
  349.2 10.1 %fusion.104 = f32[8,128]{1,0:T(8,128)S(1)} fusion(f32[8,128,4224]{2,1,0:T(8,128)} %get-tuple-element.224, f32[8,128]{1,0:T(8,128)S(1)} %get-tuple-element.225, pred[128,4224]{1,0:T(8,128)(4,1)S(1)} %iota_compare_fusion.7), kind=kLoop, calls=%fused_computation.9.clone.1 | loop fusion | flops 17300480 | bytes 17850368 | tf_op jit(solution)/shard_map/while/body/eval_jaxpr/reduce_sum | solution.py:50
  359.3 8.3 %fusion.105 = bf16[4,8,128,128]{3,2,1,0:T(8,128)(2,1)S(1)} fusion(bf16[4,8,128,128]{3,2,1,0:T(8,128)(2,1)S(1)} %get-tuple-element.242, s32[]{:T(128)S(6)} %copy.145, bf16[4,4224,128]{2,1,0:T(8,128)(2,1)} %get-tuple-element.252, f32[8,128,4224]{2,1,0:T(8,128)} %get-tuple-element.224, f32[8,128]{1,0:T(8,128)S(1)} %get-tuple-element.225, ...), kind=kOutput, calls=%fused_computation.22.clone.1 | convolution fusion | flops 1124859904 | bytes 19194880 | tf_op jit(solution)/shard_map/while/body/eval_jaxpr/gts,sd->gtd/dot_general | solution.py:51
  367.9 9.0 %fusion.103 = (f32[8,128]{1,0:T(8,128)S(1)}, f32[8,128,4224]{2,1,0:T(8,128)}) fusion(pred[128,4224]{1,0:T(8,128)(4,1)S(1)} %iota_compare_fusion.7, bf16[4,4224,128]{2,1,0:T(8,128)(2,1)} %get-tuple-element.251, s32[]{:T(128)S(6)} %copy.145, bf16[4,8,128,128]{3,2,1,0:T(8,128)(2,1)S(1)} %get-tuple-element.250), kind=kOutput, calls=%fused_computation.8.clone.1 | convolution fusion | flops 1120271360 | bytes 19190784 | tf_op jit(solution)/shard_map/while/body/eval_jaxpr/gtd,sd->gts/dot_general | solution.py:44
  376.9 10.1 %fusion.104 = f32[8,128]{1,0:T(8,128)S(1)} fusion(f32[8,128,4224]{2,1,0:T(8,128)} %get-tuple-element.224, f32[8,128]{1,0:T(8,128)S(1)} %get-tuple-element.225, pred[128,4224]{1,0:T(8,128)(4,1)S(1)} %iota_compare_fusion.7), kind=kLoop, calls=%fused_computation.9.clone.1 | loop fusion | flops 17300480 | bytes 17850368 | tf_op jit(solution)/shard_map/while/body/eval_jaxpr/reduce_sum | solution.py:50
  387.0 8.3 %fusion.105 = bf16[4,8,128,128]{3,2,1,0:T(8,128)(2,1)S(1)} fusion(bf16[4,8,128,128]{3,2,1,0:T(8,128)(2,1)S(1)} %get-tuple-element.242, s32[]{:T(128)S(6)} %copy.145, bf16[4,4224,128]{2,1,0:T(8,128)(2,1)} %get-tuple-element.252, f32[8,128,4224]{2,1,0:T(8,128)} %get-tuple-element.224, f32[8,128]{1,0:T(8,128)S(1)} %get-tuple-element.225, ...), kind=kOutput, calls=%fused_computation.22.clone.1 | convolution fusion | flops 1124859904 | bytes 19194880 | tf_op jit(solution)/shard_map/while/body/eval_jaxpr/gts,sd->gtd/dot_general | solution.py:51
  395.6 9.0 %fusion.103 = (f32[8,128]{1,0:T(8,128)S(1)}, f32[8,128,4224]{2,1,0:T(8,128)}) fusion(pred[128,4224]{1,0:T(8,128)(4,1)S(1)} %iota_compare_fusion.7, bf16[4,4224,128]{2,1,0:T(8,128)(2,1)} %get-tuple-element.251, s32[]{:T(128)S(6)} %copy.145, bf16[4,8,128,128]{3,2,1,0:T(8,128)(2,1)S(1)} %get-tuple-element.250), kind=kOutput, calls=%fused_computation.8.clone.1 | convolution fusion | flops 1120271360 | bytes 19190784 | tf_op jit(solution)/shard_map/while/body/eval_jaxpr/gtd,sd->gts/dot_general | solution.py:44
  404.6 10.1 %fusion.104 = f32[8,128]{1,0:T(8,128)S(1)} fusion(f32[8,128,4224]{2,1,0:T(8,128)} %get-tuple-element.224, f32[8,128]{1,0:T(8,128)S(1)} %get-tuple-element.225, pred[128,4224]{1,0:T(8,128)(4,1)S(1)} %iota_compare_fusion.7), kind=kLoop, calls=%fused_computation.9.clone.1 | loop fusion | flops 17300480 | bytes 17850368 | tf_op jit(solution)/shard_map/while/body/eval_jaxpr/reduce_sum | solution.py:50
  414.7 8.3 %fusion.105 = bf16[4,8,128,128]{3,2,1,0:T(8,128)(2,1)S(1)} fusion(bf16[4,8,128,128]{3,2,1,0:T(8,128)(2,1)S(1)} %get-tuple-element.242, s32[]{:T(128)S(6)} %copy.145, bf16[4,4224,128]{2,1,0:T(8,128)(2,1)} %get-tuple-element.252, f32[8,128,4224]{2,1,0:T(8,128)} %get-tuple-element.224, f32[8,128]{1,0:T(8,128)S(1)} %get-tuple-element.225, ...), kind=kOutput, calls=%fused_computation.22.clone.1 | convolution fusion | flops 1124859904 | bytes 19194880 | tf_op jit(solution)/shard_map/while/body/eval_jaxpr/gts,sd->gtd/dot_general | solution.py:51
  423.3 9.0 %fusion.103 = (f32[8,128]{1,0:T(8,128)S(1)}, f32[8,128,4224]{2,1,0:T(8,128)}) fusion(pred[128,4224]{1,0:T(8,128)(4,1)S(1)} %iota_compare_fusion.7, bf16[4,4224,128]{2,1,0:T(8,128)(2,1)} %get-tuple-element.251, s32[]{:T(128)S(6)} %copy.145, bf16[4,8,128,128]{3,2,1,0:T(8,128)(2,1)S(1)} %get-tuple-element.250), kind=kOutput, calls=%fused_computation.8.clone.1 | convolution fusion | flops 1120271360 | bytes 19190784 | tf_op jit(solution)/shard_map/while/body/eval_jaxpr/gtd,sd->gts/dot_general | solution.py:44
  432.3 10.1 %fusion.104 = f32[8,128]{1,0:T(8,128)S(1)} fusion(f32[8,128,4224]{2,1,0:T(8,128)} %get-tuple-element.224, f32[8,128]{1,0:T(8,128)S(1)} %get-tuple-element.225, pred[128,4224]{1,0:T(8,128)(4,1)S(1)} %iota_compare_fusion.7), kind=kLoop, calls=%fused_computation.9.clone.1 | loop fusion | flops 17300480 | bytes 17850368 | tf_op jit(solution)/shard_map/while/body/eval_jaxpr/reduce_sum | solution.py:50
  442.4 8.3 %fusion.105 = bf16[4,8,128,128]{3,2,1,0:T(8,128)(2,1)S(1)} fusion(bf16[4,8,128,128]{3,2,1,0:T(8,128)(2,1)S(1)} %get-tuple-element.242, s32[]{:T(128)S(6)} %copy.145, bf16[4,4224,128]{2,1,0:T(8,128)(2,1)} %get-tuple-element.252, f32[8,128,4224]{2,1,0:T(8,128)} %get-tuple-element.224, f32[8,128]{1,0:T(8,128)S(1)} %get-tuple-element.225, ...), kind=kOutput, calls=%fused_computation.22.clone.1 | convolution fusion | flops 1124859904 | bytes 19194880 | tf_op jit(solution)/shard_map/while/body/eval_jaxpr/gts,sd->gtd/dot_general | solution.py:51
  452.3 2.5 slice.72
  457.1 2.5 slice.76
  465.7 3.2 maximum_bitcast_fusion
  469.1 120.3 %while.23 = (s32[]{:T(128)}, bf16[4,8,128,128]{3,2,1,0:T(8,128)(2,1)S(1)}, bf16[4,8,128,128]{3,2,1,0:T(8,128)(2,1)}, bf16[4,4352,128]{2,1,0:T(8,128)(2,1)}, bf16...) while((s32[]{:T(128)}, bf16[4,8,128,128]{3,2,1,0:T(8,128)(2,1)S(1)}, ...), condition=%wide.region_14.15_spmd.clone, body=%wide.region_11.14_spmd.clone.sunk | while | flops 2331539456 | bytes 58498132 | solution.py:59
  469.4 10.8 %fusion.108 = (f32[8,128]{1,0:T(8,128)S(1)}, f32[8,128,4352]{2,1,0:T(8,128)}) fusion(pred[128,4352]{1,0:T(8,128)(4,1)S(1)} %iota_compare_fusion.8, bf16[4,4352,128]{2,1,0:T(8,128)(2,1)} %get-tuple-element.272, s32[]{:T(128)S(6)} %copy.151, bf16[4,8,128,128]{3,2,1,0:T(8,128)(2,1)} %get-tuple-element.271), kind=kOutput, calls=%fused_computation.31.clone.1 | convolution fusion | flops 1154219008 | bytes 19764224 | tf_op jit(solution)/shard_map/while/body/eval_jaxpr/gtd,sd->gts/dot_general | solution.py:44
  480.2 10.4 %fusion.109 = f32[8,128]{1,0:T(8,128)S(1)} fusion(f32[8,128,4352]{2,1,0:T(8,128)} %get-tuple-element.232, f32[8,128]{1,0:T(8,128)S(1)} %get-tuple-element.233, pred[128,4352]{1,0:T(8,128)(4,1)S(1)} %iota_compare_fusion.8), kind=kLoop, calls=%fused_computation.32.clone.1 | loop fusion | flops 17824768 | bytes 18391040 | tf_op jit(solution)/shard_map/while/body/eval_jaxpr/reduce_sum | solution.py:50
  490.6 8.5 %fusion.110 = bf16[4,8,128,128]{3,2,1,0:T(8,128)(2,1)S(1)} fusion(bf16[4,8,128,128]{3,2,1,0:T(8,128)(2,1)S(1)} %get-tuple-element.263, s32[]{:T(128)S(6)} %copy.151, bf16[4,4352,128]{2,1,0:T(8,128)(2,1)} %get-tuple-element.273, f32[8,128,4352]{2,1,0:T(8,128)} %get-tuple-element.232, f32[8,128]{1,0:T(8,128)S(1)} %get-tuple-element.233, ...), kind=kOutput, calls=%fused_computation.45.clone.1 | convolution fusion | flops 1158938624 | bytes 19768320 | tf_op jit(solution)/shard_map/while/body/eval_jaxpr/gts,sd->gtd/dot_general | solution.py:51
  499.4 10.8 %fusion.108 = (f32[8,128]{1,0:T(8,128)S(1)}, f32[8,128,4352]{2,1,0:T(8,128)}) fusion(pred[128,4352]{1,0:T(8,128)(4,1)S(1)} %iota_compare_fusion.8, bf16[4,4352,128]{2,1,0:T(8,128)(2,1)} %get-tuple-element.272, s32[]{:T(128)S(6)} %copy.151, bf16[4,8,128,128]{3,2,1,0:T(8,128)(2,1)} %get-tuple-element.271), kind=kOutput, calls=%fused_computation.31.clone.1 | convolution fusion | flops 1154219008 | bytes 19764224 | tf_op jit(solution)/shard_map/while/body/eval_jaxpr/gtd,sd->gts/dot_general | solution.py:44
  510.3 10.4 %fusion.109 = f32[8,128]{1,0:T(8,128)S(1)} fusion(f32[8,128,4352]{2,1,0:T(8,128)} %get-tuple-element.232, f32[8,128]{1,0:T(8,128)S(1)} %get-tuple-element.233, pred[128,4352]{1,0:T(8,128)(4,1)S(1)} %iota_compare_fusion.8), kind=kLoop, calls=%fused_computation.32.clone.1 | loop fusion | flops 17824768 | bytes 18391040 | tf_op jit(solution)/shard_map/while/body/eval_jaxpr/reduce_sum | solution.py:50
  520.7 8.5 %fusion.110 = bf16[4,8,128,128]{3,2,1,0:T(8,128)(2,1)S(1)} fusion(bf16[4,8,128,128]{3,2,1,0:T(8,128)(2,1)S(1)} %get-tuple-element.263, s32[]{:T(128)S(6)} %copy.151, bf16[4,4352,128]{2,1,0:T(8,128)(2,1)} %get-tuple-element.273, f32[8,128,4352]{2,1,0:T(8,128)} %get-tuple-element.232, f32[8,128]{1,0:T(8,128)S(1)} %get-tuple-element.233, ...), kind=kOutput, calls=%fused_computation.45.clone.1 | convolution fusion | flops 1158938624 | bytes 19768320 | tf_op jit(solution)/shard_map/while/body/eval_jaxpr/gts,sd->gtd/dot_general | solution.py:51
  529.5 10.8 %fusion.108 = (f32[8,128]{1,0:T(8,128)S(1)}, f32[8,128,4352]{2,1,0:T(8,128)}) fusion(pred[128,4352]{1,0:T(8,128)(4,1)S(1)} %iota_compare_fusion.8, bf16[4,4352,128]{2,1,0:T(8,128)(2,1)} %get-tuple-element.272, s32[]{:T(128)S(6)} %copy.151, bf16[4,8,128,128]{3,2,1,0:T(8,128)(2,1)} %get-tuple-element.271), kind=kOutput, calls=%fused_computation.31.clone.1 | convolution fusion | flops 1154219008 | bytes 19764224 | tf_op jit(solution)/shard_map/while/body/eval_jaxpr/gtd,sd->gts/dot_general | solution.py:44
  540.3 10.4 %fusion.109 = f32[8,128]{1,0:T(8,128)S(1)} fusion(f32[8,128,4352]{2,1,0:T(8,128)} %get-tuple-element.232, f32[8,128]{1,0:T(8,128)S(1)} %get-tuple-element.233, pred[128,4352]{1,0:T(8,128)(4,1)S(1)} %iota_compare_fusion.8), kind=kLoop, calls=%fused_computation.32.clone.1 | loop fusion | flops 17824768 | bytes 18391040 | tf_op jit(solution)/shard_map/while/body/eval_jaxpr/reduce_sum | solution.py:50
  550.7 8.5 %fusion.110 = bf16[4,8,128,128]{3,2,1,0:T(8,128)(2,1)S(1)} fusion(bf16[4,8,128,128]{3,2,1,0:T(8,128)(2,1)S(1)} %get-tuple-element.263, s32[]{:T(128)S(6)} %copy.151, bf16[4,4352,128]{2,1,0:T(8,128)(2,1)} %get-tuple-element.273, f32[8,128,4352]{2,1,0:T(8,128)} %get-tuple-element.232, f32[8,128]{1,0:T(8,128)S(1)} %get-tuple-element.233, ...), kind=kOutput, calls=%fused_computation.45.clone.1 | convolution fusion | flops 1158938624 | bytes 19768320 | tf_op jit(solution)/shard_map/while/body/eval_jaxpr/gts,sd->gtd/dot_general | solution.py:51
  559.6 10.8 %fusion.108 = (f32[8,128]{1,0:T(8,128)S(1)}, f32[8,128,4352]{2,1,0:T(8,128)}) fusion(pred[128,4352]{1,0:T(8,128)(4,1)S(1)} %iota_compare_fusion.8, bf16[4,4352,128]{2,1,0:T(8,128)(2,1)} %get-tuple-element.272, s32[]{:T(128)S(6)} %copy.151, bf16[4,8,128,128]{3,2,1,0:T(8,128)(2,1)} %get-tuple-element.271), kind=kOutput, calls=%fused_computation.31.clone.1 | convolution fusion | flops 1154219008 | bytes 19764224 | tf_op jit(solution)/shard_map/while/body/eval_jaxpr/gtd,sd->gts/dot_general | solution.py:44
  570.4 10.4 %fusion.109 = f32[8,128]{1,0:T(8,128)S(1)} fusion(f32[8,128,4352]{2,1,0:T(8,128)} %get-tuple-element.232, f32[8,128]{1,0:T(8,128)S(1)} %get-tuple-element.233, pred[128,4352]{1,0:T(8,128)(4,1)S(1)} %iota_compare_fusion.8), kind=kLoop, calls=%fused_computation.32.clone.1 | loop fusion | flops 17824768 | bytes 18391040 | tf_op jit(solution)/shard_map/while/body/eval_jaxpr/reduce_sum | solution.py:50
  580.8 8.5 %fusion.110 = bf16[4,8,128,128]{3,2,1,0:T(8,128)(2,1)S(1)} fusion(bf16[4,8,128,128]{3,2,1,0:T(8,128)(2,1)S(1)} %get-tuple-element.263, s32[]{:T(128)S(6)} %copy.151, bf16[4,4352,128]{2,1,0:T(8,128)(2,1)} %get-tuple-element.273, f32[8,128,4352]{2,1,0:T(8,128)} %get-tuple-element.232, f32[8,128]{1,0:T(8,128)S(1)} %get-tuple-element.233, ...), kind=kOutput, calls=%fused_computation.45.clone.1 | convolution fusion | flops 1158938624 | bytes 19768320 | tf_op jit(solution)/shard_map/while/body/eval_jaxpr/gts,sd->gtd/dot_general | solution.py:51
  (90 shorter events, 33.2 us)
Async XLA Ops:
  17.4 100.6 %all-to-all-start = ((bf16[8,4,128,4,128]{4,2,1,3,0:T(8,128)(2,1)}), bf16[8,4,128,4,128]{4,2,1,3,0:T(8,128)(2,1)}, u32[]{:S(2)}, u32[]{:S(2)}) async-start(bf16[8,4,128,4,128]{4,2,1,3,0:T(8,128)(2,1)} %copy.105), calls=%async_computation | async-start | bytes 8388608 | tf_op jit(solution)/shard_map/all_to_all | solution.py:116
  37.8 84.7 %copy-start.9 = (bf16[1,128,4,128]{3,2,1,0:T(4,128)(2,1)S(1)}, bf16[1,128,4,128]{3,2,1,0:T(4,128)(2,1)}, u32[]{:S(2)}) copy-start(bf16[1,128,4,128]{3,2,1,0:T(4,128)(2,1)} %param.17) | copy-start | bytes 393220
  117.9 97.1 %all-to-all-start.1 = ((bf16[8,4,128,4,128]{4,2,1,3,0:T(8,128)(2,1)}), bf16[8,4,128,4,128]{4,2,1,3,0:T(8,128)(2,1)}, u32[]{:S(2)}, u32[]{:S(2)}) async-start(bf16[8,4,128,4,128]{4,2,1,3,0:T(8,128)(2,1)} %copy.109), calls=%async_computation.1 | async-start | bytes 8388608 | tf_op jit(solution)/shard_map/all_to_all | solution.py:117
  131.0 3.4 copy-start.11
  131.0 4.0 copy-start.7
  131.0 4.3 copy-start.12
  215.1 119.7 %all-to-all-start.2 = ((bf16[8,5,128,4,128]{4,2,1,3,0:T(8,128)(2,1)}), bf16[8,5,128,4,128]{4,2,1,3,0:T(8,128)(2,1)}, u32[]{:S(2)}, u32[]{:S(2)}) async-start(bf16[8,5,128,4,128]{4,2,1,3,0:T(8,128)(2,1)} %copy.117), calls=%async_computation.2 | async-start | bytes 10485760 | tf_op jit(solution)/shard_map/all_to_all | solution.py:125
  219.9 8.1 %copy-start.2 = (bf16[1,128,32,128]{3,2,1,0:T(8,128)(2,1)S(1)}, bf16[1,128,32,128]{3,2,1,0:T(8,128)(2,1)}, u32[]{:S(2)}) copy-start(bf16[1,128,32,128]{3,2,1,0:T(8,128)(2,1)} %param.18) | copy-start | bytes 3145732
  231.7 1.7 copy-start.10
  231.7 2.3 copy-start.1
  239.1 2.7 copy-start.8
  334.8 122.3 %all-to-all-start.3 = ((bf16[8,5,128,4,128]{4,2,1,3,0:T(8,128)(2,1)}), bf16[8,5,128,4,128]{4,2,1,3,0:T(8,128)(2,1)}, u32[]{:S(2)}, u32[]{:S(2)}) async-start(bf16[8,5,128,4,128]{4,2,1,3,0:T(8,128)(2,1)} %copy.121), calls=%async_computation.3 | async-start | bytes 10485760 | tf_op jit(solution)/shard_map/all_to_all | solution.py:126
  459.6 1.7 copy-start.6
  461.3 4.3 copy-start
  461.3 4.3 copy-start.4
  461.3 4.3 copy-start.5
  465.7 3.4 copy-start.3
where the time goes:
time: 601 us; the launch traced here: 591 us
  waiting for transfers between devices  238 us (40%)
  matrix products  147 us (24%)
  other arithmetic  111 us (18%)
  local copies, waits for them, and re-layouts  72.9 us (12%)
  starting transfers between devices  21.5 us (4%)
    all_to_all x1, waiting for transfers between devices, local(): lax.all_to_all(send_keys_two, 'node', split_axis=0, concat_axis=0, tiled=...  82 us
    reduce_sum x8, other arithmetic, one_head(): total_weight = jnp.sum(weights, axis=-1, keepdims=True)  81.9 us
    all_to_all x1, waiting for transfers between devices, local(): lax.all_to_all(send_keys_one, 'node', split_axis=0, concat_axis=0, tiled=...  80.1 us
    dot_general x8, matrix products, one_head(): jnp.einsum('gtd,sd->gts', query_head, key_head, preferred_element_type=jn...  79.2 us
    all_to_all x1, waiting for transfers between devices, local(): lax.all_to_all(send_values_one, 'node', split_axis=0, concat_axis=0, tile...  75.7 us
    dot_general x8, matrix products, one_head(): jnp.einsum('gts,sd->gtd', weights.astype(jnp.bfloat16), value_head, prefe...  67.4 us
    gather x8, local copies, waits for them, and re-layouts, outgoing(): return (cache_keys[block_index], cache_values[block_index])  47.1 us
  transfers between devices with their start and end apart: 4, of which 3 were waited for; matrix products, arithmetic and copies ran while one was open for 30% of the time, Pallas kernels for 0%

commit v1 on v0

v1 whole, which is shorter than its diff:
```python
import functools

import jax
import jax.numpy as jnp
from jax import lax
from jax.experimental import pallas as pl
from jax.experimental.pallas import tpu as pltpu
from jax.sharding import PartitionSpec as P

rope_theta = 500000.0
log2_e = 1.4426950408889634
stat_rows = 32
row_tile = 256
vmem_bytes = 56 * 1024 * 1024


def rotary(vector, position_row):
    head_width = vector.shape[-1]
    half_width = head_width // 2
    frequency = rope_theta ** (-(jnp.arange(half_width, dtype=jnp.float32) * 2.0) / head_width)
    angles = position_row.astype(jnp.float32)[:, None] * frequency[None, :]
    cosine = jnp.cos(angles)[:, None, :]
    sine_part = jnp.sin(angles)[:, None, :]
    widened = vector.astype(jnp.float32)
    first_half = widened[..., :half_width]
    second_half = widened[..., half_width:]
    turned = jnp.concatenate(
        [
            first_half * cosine - second_half * sine_part,
            second_half * cosine + first_half * sine_part,
        ],
        -1,
    )
    return turned.astype(jnp.bfloat16)


def local_blocks(paths, here_index, per_owner, per_peer):
    is_local = paths // per_owner == here_index
    slot_rank = jnp.cumsum(is_local.astype(jnp.int32), axis=1) - 1
    slot_range = jnp.arange(per_peer, dtype=jnp.int32)
    selected = jnp.logical_and(
        is_local[:, :, None], slot_rank[:, :, None] == slot_range[None, None, :]
    )
    return jnp.sum(jnp.where(selected, (paths % per_owner)[:, :, None], 0), axis=1)


def pack_kernel(per_peer, head_count, token_count, with_new, index_ref, head_ref, *refs):
    key_refs = refs[:per_peer]
    value_refs = refs[per_peer : 2 * per_peer]
    refs = refs[2 * per_peer :]
    new_refs = ()
    if with_new:
        new_refs, refs = refs[:2], refs[2:]
    out_refs, wide = refs[:head_count], refs[head_count]
    step = pl.program_id(0)
    mine = head_ref[0]
    span_rows = 2 * per_peer * token_count

    def spread(rows, offset):
        wide[...] = rows.astype(jnp.float32)
        for far in range(head_count):
            head = lax.bitwise_xor(mine, far)
            picked = wide[pl.ds(head, token_count, stride=head_count), :]
            out_refs[far][pl.ds(offset, token_count), :] = picked.astype(jnp.bfloat16)

    for which, source_refs in enumerate((key_refs, value_refs)):
        for slot, source in enumerate(source_refs):
            offset = step * span_rows + (which * per_peer + slot) * token_count
            spread(source[0], pl.multiple_of(offset, token_count))
    if with_new:

        @pl.when(step == 0)
        def _():
            base = pl.num_programs(0) * span_rows
            for which, source in enumerate(new_refs):
                spread(source[...], pl.multiple_of(base + which * token_count, token_count))


def pack(cache_keys, cache_values, block_index, head_index, new_rows, per_peer):
    block_count, token_count, head_count, width = cache_keys.shape
    path_count = block_index.shape[0]
    flat_keys = cache_keys.reshape(block_count, token_count * head_count, width)
    flat_values = cache_values.reshape(block_count, token_count * head_count, width)
    span_rows = 2 * per_peer * token_count
    out_rows = path_count * span_rows + (2 * token_count if new_rows else 0)

    def block_spec(slot):
        return pl.BlockSpec(
            (1, token_count * head_count, width),
            lambda step, index, head: (index[step * per_peer + slot], 0, 0),
        )

    cache_specs = [block_spec(slot) for slot in range(per_peer)]
    new_spec = pl.BlockSpec((token_count * head_count, width), lambda step, index, head: (0, 0))
    operands = [flat_keys] * per_peer + [flat_values] * per_peer
    operands += [row.reshape(token_count * head_count, width) for row in new_rows]
    return pl.pallas_call(
        functools.partial(pack_kernel, per_peer, head_count, token_count, bool(new_rows)),
        grid_spec=pltpu.PrefetchScalarGridSpec(
            num_scalar_prefetch=2,
            grid=(path_count,),
            in_specs=cache_specs + cache_specs + [new_spec] * len(new_rows),
            out_specs=[pl.BlockSpec((out_rows, width), lambda step, index, head: (0, 0))]
            * head_count,
            scratch_shapes=[pltpu.VMEM((token_count * head_count, width), jnp.float32)],
        ),
        out_shape=[jax.ShapeDtypeStruct((out_rows, width), jnp.bfloat16)] * head_count,
        compiler_params=pltpu.CompilerParams(vmem_limit_bytes=vmem_bytes),
        cost_estimate=pl.CostEstimate(
            flops=0, bytes_accessed=4 * head_count * out_rows * width, transcendentals=0
        ),
        name="pack_rows",
    )(block_index.reshape(-1), head_index, *operands)


def eye(size):
    return lax.broadcasted_iota(jnp.int32, (size, size), 0) == lax.broadcasted_iota(
        jnp.int32, (size, size), 1
    )


def product(left, right):
    return lax.dot_general(
        left, right, (((1,), (1,)), ((), ())), preferred_element_type=jnp.float32
    )


def attend_rows(query, key_parts, value_parts, mask, score_scale):
    scores = [product(query, keys) for keys in key_parts]
    if mask is not None:
        scores[-1] = jnp.where(mask, scores[-1], -1e30)
    row_max = functools.reduce(
        jnp.maximum, [jnp.max(part, axis=-1, keepdims=True) for part in scores]
    )
    total = jnp.zeros_like(row_max)
    mixture = jnp.zeros((query.shape[0], value_parts[0].shape[-1]), jnp.float32)
    for part, values in zip(scores, value_parts):
        weights = jnp.exp2((part - row_max) * (score_scale * log2_e))
        total = total + jnp.sum(weights, axis=-1, keepdims=True)
        mixture = mixture + jnp.dot(
            weights.astype(jnp.bfloat16), values, preferred_element_type=jnp.float32
        )
    return mixture / total, row_max * score_scale + jnp.log(total)


def store_partial(out_ref, tile, mixture, level, lanes):
    rows = mixture.shape[0]
    out_ref[0, pl.ds(pl.multiple_of(tile * rows, rows), rows), :] = mixture.astype(jnp.bfloat16)
    picks = eye(lanes)
    flat = [
        jnp.sum(
            jnp.where(picks, level[part * lanes : (part + 1) * lanes], 0.0), axis=0, keepdims=True
        )
        for part in range(rows // lanes)
    ]
    return flat


def store_stats(out_ref, levels):
    row_count = out_ref.shape[1] - stat_rows
    high = levels.astype(jnp.bfloat16).astype(jnp.float32)
    middle = (levels - high).astype(jnp.bfloat16).astype(jnp.float32)
    low = levels - high - middle
    stats = jnp.concatenate([high, middle, low, jnp.zeros_like(levels)], 0)
    out_ref[0, pl.ds(row_count, stat_rows), :] = stats.astype(jnp.bfloat16)


def attend_task(query_ref, out_ref, level_ref, key_parts, value_parts, mask_of, score_scale):
    row_count = out_ref.shape[1] - stat_rows
    lanes = out_ref.shape[2]
    per_tile = row_tile // lanes

    def tile_step(tile, carry):
        query = query_ref[0, pl.ds(pl.multiple_of(tile * row_tile, row_tile), row_tile), :]
        mixture, level = attend_rows(
            query,
            [read() for read in key_parts],
            [read() for read in value_parts],
            None if mask_of is None else mask_of(tile),
            score_scale,
        )
        flat = store_partial(out_ref, tile, mixture, level, lanes)
        for part in range(per_tile):
            level_ref[pl.ds(tile * per_tile + part, 1), :] = flat[part]
        return carry

    lax.fori_loop(0, row_count // row_tile, tile_step, 0)
    store_stats(out_ref, level_ref[...])


def part_readers(refs, part_rows):
    keys = [functools.partial(lambda ref: ref[pl.ds(0, part_rows), :], ref) for ref in refs]
    values = [
        functools.partial(lambda ref: ref[pl.ds(part_rows, part_rows), :], ref) for ref in refs
    ]
    return keys, values


def first_kernel(source_count, part_rows, score_scale, has_base, query_ref, *refs):
    source_refs = refs[:source_count]
    out_ref, level_ref = refs[source_count + has_base :]
    keys, values = part_readers(source_refs, part_rows)
    attend_task(query_ref, out_ref, level_ref, keys, values, None, score_scale)


def attend_first(queries, sources, base, first_path, path_count, part_rows, score_scale):
    span_count, row_count, width = queries.shape
    span_rows = 2 * part_rows
    out_shape = jax.ShapeDtypeStruct((span_count, row_count + stat_rows, width), jnp.bfloat16)
    has_base = int(base is not None)
    operands = [queries, *sources] + ([base] if has_base else [])
    keys = len(sources) * part_rows
    return pl.pallas_call(
        functools.partial(first_kernel, len(sources), part_rows, score_scale, has_base),
        grid=(path_count,),
        in_specs=[pl.BlockSpec((1, row_count, width), lambda step: (first_path + step, 0, 0))]
        + [pl.BlockSpec((span_rows, width), lambda step: (step, 0))] * len(sources)
        + [pl.BlockSpec(memory_space=pl.ANY)] * has_base,
        out_specs=pl.BlockSpec(
            (1, row_count + stat_rows, width), lambda step: (first_path + step, 0, 0)
        ),
        out_shape=out_shape,
        scratch_shapes=[pltpu.VMEM((row_count // width, width), jnp.float32)],
        input_output_aliases={len(operands) - 1: 0} if has_base else {},
        compiler_params=pltpu.CompilerParams(vmem_limit_bytes=vmem_bytes),
        cost_estimate=pl.CostEstimate(
            flops=8 * path_count * row_count * keys * width,
            bytes_accessed=4 * path_count * (row_count + keys) * width,
            transcendentals=path_count * row_count * keys,
        ),
        name="attend_first",
    )(*operands)


def second_kernel(
    chunk_count, source_count, chunk_paths, part_rows, score_scale, parent_ref, group_ref, *refs
):
    query_ref = refs[0]
    source_refs = refs[1 : 1 + chunk_count * source_count]
    out_ref, level_ref, held, fresh, semaphores = refs[1 + chunk_count * source_count :]
    span_rows = 2 * part_rows
    token_count = fresh.shape[1] // 2
    step = pl.program_id(0)

    def copies():
        out = []
        for chunk in range(chunk_count):
            for source in range(source_count):
                ref = source_refs[chunk * source_count + source]
                for path in range(chunk_paths):
                    out.append(
                        pltpu.make_async_copy(
                            ref.at[pl.ds(path * span_rows, span_rows)],
                            held.at[source, chunk * chunk_paths + path],
                            semaphores.at[len(out)],
                        )
                    )
        for source in range(source_count):
            ref = source_refs[(chunk_count - 1) * source_count + source]
            out.append(
                pltpu.make_async_copy(
                    ref.at[pl.ds(chunk_paths * span_rows, 2 * token_count)],
                    fresh.at[source],
                    semaphores.at[len(out)],
                )
            )
        return out

    @pl.when(step == 0)
    def _():
        moves = copies()
        for move in moves:
            move.start()
        for move in moves:
            move.wait()

    parent = parent_ref[step]
    home = parent // source_count
    present = home == group_ref[0]
    slot = lax.bitwise_xor(parent % source_count, group_ref[1])
    keys = [
        functools.partial(lambda source: held[source, parent, pl.ds(0, part_rows), :], source)
        for source in range(source_count)
    ]
    values = [
        functools.partial(
            lambda source: held[source, parent, pl.ds(part_rows, part_rows), :], source
        )
        for source in range(source_count)
    ]
    keys.append(lambda: fresh[slot, pl.ds(0, token_count), :])
    values.append(lambda: fresh[slot, pl.ds(token_count, token_count), :])

    def mask_of(tile):
        return jnp.broadcast_to(present, (row_tile, token_count))

    attend_task(query_ref, out_ref, level_ref, keys, values, mask_of, score_scale)


def attend_second(queries, chunks, parents, group_index, chunk_paths, part_rows, score_scale):
    span_count, row_count, width = queries.shape
    source_count = len(chunks[0])
    chunk_count = len(chunks)
    span_rows = 2 * part_rows
    fresh_rows = chunks[-1][0].shape[0] - chunk_paths * span_rows
    operands = [ref for chunk in chunks for ref in chunk]
    keys = source_count * part_rows + fresh_rows // 2
    copy_count = chunk_count * source_count * chunk_paths + source_count
    return pl.pallas_call(
        functools.partial(
            second_kernel, chunk_count, source_count, chunk_paths, part_rows, score_scale
        ),
        grid_spec=pltpu.PrefetchScalarGridSpec(
            num_scalar_prefetch=2,
            grid=(span_count,),
            in_specs=[pl.BlockSpec((1, row_count, width), lambda step, parent, group: (step, 0, 0))]
            + [pl.BlockSpec(memory_space=pl.ANY)] * len(operands),
            out_specs=pl.BlockSpec(
                (1, row_count + stat_rows, width), lambda step, parent, group: (step, 0, 0)
            ),
            scratch_shapes=[
                pltpu.VMEM((row_count // width, width), jnp.float32),
                pltpu.VMEM(
                    (source_count, chunk_count * chunk_paths, span_rows, width), jnp.bfloat16
                ),
                pltpu.VMEM((source_count, fresh_rows, width), jnp.bfloat16),
                pltpu.SemaphoreType.DMA((copy_count,)),
            ],
        ),
        out_shape=jax.ShapeDtypeStruct((span_count, row_count + stat_rows, width), jnp.bfloat16),
        compiler_params=pltpu.CompilerParams(vmem_limit_bytes=vmem_bytes),
        cost_estimate=pl.CostEstimate(
            flops=8 * span_count * row_count * keys * width,
            bytes_accessed=4 * span_count * (row_count + keys) * width,
            transcendentals=span_count * row_count * keys,
        ),
        name="attend_second",
    )(parents, group_index, queries, *operands)


def own_kernel(group_size, score_scale, query_ref, key_ref, value_ref, out_ref, level_ref):
    token_count = key_ref.shape[1]

    def mask_of(tile):
        row = tile * row_tile + lax.broadcasted_iota(jnp.int32, (row_tile, token_count), 0)
        column = lax.broadcasted_iota(jnp.int32, (row_tile, token_count), 1)
        return column * group_size <= row

    attend_task(
        query_ref,
        out_ref,
        level_ref,
        [lambda: key_ref[0]],
        [lambda: value_ref[0]],
        mask_of,
        score_scale,
    )


def attend_own(queries, keys, values, score_scale):
    head_count, token_count, width = keys.shape
    row_count = queries.shape[1]
    return pl.pallas_call(
        functools.partial(own_kernel, row_count // token_count, score_scale),
        grid=(head_count,),
        in_specs=[
            pl.BlockSpec((1, row_count, width), lambda step: (step, 0, 0)),
            pl.BlockSpec((1, token_count, width), lambda step: (step, 0, 0)),
            pl.BlockSpec((1, token_count, width), lambda step: (step, 0, 0)),
        ],
        out_specs=pl.BlockSpec((1, row_count + stat_rows, width), lambda step: (step, 0, 0)),
        out_shape=jax.ShapeDtypeStruct((head_count, row_count + stat_rows, width), jnp.bfloat16),
        scratch_shapes=[pltpu.VMEM((row_count // width, width), jnp.float32)],
        compiler_params=pltpu.CompilerParams(vmem_limit_bytes=vmem_bytes),
        cost_estimate=pl.CostEstimate(
            flops=8 * head_count * row_count * token_count * width,
            bytes_accessed=4 * head_count * (row_count + token_count) * width,
            transcendentals=head_count * row_count * token_count,
        ),
        name="attend_own",
    )(queries, keys, values)


def merge_kernel(head_count, group_size, part_ref, own_ref, part_stat_ref, own_stat_ref, out_ref):
    token_tile, _, lanes = out_ref.shape[1:]
    rows = token_tile * group_size
    stat_tile = rows // lanes
    step = pl.program_id(0)
    group_count = part_ref.shape[0] // head_count
    picks = eye(lanes)

    def levels(ref, place):
        stats = ref[place].astype(jnp.float32)
        span = stat_rows // 4
        return stats[:span] + stats[span : 2 * span] + stats[2 * span : 3 * span]

    heads = []
    for head in range(head_count):
        places = [(part_ref, part_stat_ref, group * head_count + head) for group in range(group_count)]
        places.append((own_ref, own_stat_ref, head))
        level = [levels(stat, place) for _, stat, place in places]
        top = functools.reduce(jnp.maximum, level)
        shares = [jnp.exp(one - top) for one in level]
        total = functools.reduce(jnp.add, shares)
        shares = [one / total for one in shares]
        pieces = []
        for part in range(stat_tile):
            mixed = None
            for (ref, _, place), share in zip(places, shares):
                span = lax.broadcasted_iota(jnp.int32, share.shape, 0) == step * stat_tile + part
                line = jnp.sum(jnp.where(span, share, 0.0), axis=0, keepdims=True)
                column = jnp.sum(jnp.where(picks, line, 0.0), axis=1, keepdims=True)
                block = ref[place, pl.ds(part * lanes, lanes), :].astype(jnp.float32) * column
                mixed = block if mixed is None else mixed + block
            pieces.append(mixed.reshape(lanes // group_size, group_size, lanes))
        heads.append(jnp.concatenate(pieces, 0))
    out_ref[0] = jnp.concatenate(heads, 1).astype(out_ref.dtype)


def merge(parts, own, token_count):
    part_count, padded_rows, width = parts.shape
    head_count = own.shape[0]
    row_count = padded_rows - stat_rows
    group_size = row_count // token_count
    token_tile = 32
    rows = token_tile * group_size
    stat_block = row_count // stat_rows
    return pl.pallas_call(
        functools.partial(merge_kernel, head_count, group_size),
        grid=(token_count // token_tile,),
        in_specs=[
            pl.BlockSpec((part_count, rows, width), lambda step: (0, step, 0)),
            pl.BlockSpec((head_count, rows, width), lambda step: (0, step, 0)),
            pl.BlockSpec((part_count, stat_rows, width), lambda step: (0, stat_block, 0)),
            pl.BlockSpec((head_count, stat_rows, width), lambda step: (0, stat_block, 0)),
        ],
        out_specs=pl.BlockSpec(
            (1, token_tile, head_count * group_size, width), lambda step: (0, step, 0, 0)
        ),
        out_shape=jax.ShapeDtypeStruct(
            (1, token_count, head_count * group_size, width), jnp.bfloat16
        ),
        compiler_params=pltpu.CompilerParams(vmem_limit_bytes=vmem_bytes),
        cost_estimate=pl.CostEstimate(
            flops=4 * part_count * row_count * width,
            bytes_accessed=4 * part_count * row_count * width,
            transcendentals=0,
        ),
        name="merge_parts",
    )(parts, own, parts, own)


def local(
    chunk_count,
    queries_one,
    keys_one,
    values_one,
    queries_two,
    keys_two,
    values_two,
    cache_keys,
    cache_values,
    paths,
    parents,
    positions,
):
    here_index = lax.axis_index("node")
    peer_count = lax.axis_size("node")
    block_count, token_count, head_count, width = cache_keys.shape
    per_peer = paths.shape[1] // peer_count
    group_size = queries_one.shape[2] // head_count
    copies = peer_count // head_count
    score_scale = width ** (-0.5)
    my_head = here_index % head_count
    my_group = here_index // head_count

    def by_head(rotated):
        split = rotated.reshape(token_count, head_count, group_size, width)
        rows = jnp.moveaxis(split, 1, 0).reshape(head_count, token_count * group_size, width)
        return jnp.tile(rows, (copies, 1, 1))

    def exchange(rows):
        return lax.all_to_all(rows, "node", split_axis=0, concat_axis=0, tiled=True)

    send_one = by_head(rotary(queries_one[0], positions[0, 0]))
    got_one = exchange(send_one)
    key_rot_one = rotary(keys_one[0], positions[0, 0])
    key_rot_two = rotary(keys_two[0], positions[1, 0])

    block_index = local_blocks(paths, here_index, block_count, per_peer)
    chunk_paths = peer_count // chunk_count
    part_rows = per_peer * token_count
    chunks = []
    for chunk in range(chunk_count):
        last = chunk == chunk_count - 1
        packed = pack(
            cache_keys,
            cache_values,
            block_index[chunk * chunk_paths : (chunk + 1) * chunk_paths],
            my_head[None],
            (key_rot_one, values_one[0]) if last else (),
            per_peer,
        )
        arrived = [packed[0]]
        for far in range(1, head_count):
            pairs = [(node, node ^ far) for node in range(peer_count)]
            arrived.append(lax.ppermute(packed[far], "node", pairs))
        chunks.append(arrived)

    send_two = by_head(rotary(queries_two[0], positions[1, 0]))
    got_two = exchange(send_two)

    own_one = attend_own(
        send_one, jnp.moveaxis(key_rot_one, 1, 0), jnp.moveaxis(values_one[0], 1, 0), score_scale
    )
    own_two = attend_own(
        send_two, jnp.moveaxis(key_rot_two, 1, 0), jnp.moveaxis(values_two[0], 1, 0), score_scale
    )

    partial_one = None
    for chunk in range(chunk_count):
        partial_one = attend_first(
            got_one,
            chunks[chunk],
            partial_one,
            chunk * chunk_paths,
            chunk_paths,
            part_rows,
            score_scale,
        )
    parts_one = exchange(partial_one)
    partial_two = attend_second(
        got_two,
        chunks,
        parents,
        jnp.stack([my_group, my_head]),
        chunk_paths,
        part_rows,
        score_scale,
    )
    parts_two = exchange(partial_two)
    return merge(parts_one, own_one, token_count), merge(parts_two, own_two, token_count)


def solution(mesh):
    in_specs = (
        P(("group", "node"), None, "head", None),
        P(("group", "node"), None, "head", None),
        P(("group", "node"), None, "head", None),
        P(("group", "node"), None, "head", None),
        P(("group", "node"), None, "head", None),
        P(("group", "node"), None, "head", None),
        P(("group", "node"), None, "head", None),
        P(("group", "node"), None, "head", None),
        P("group", None),
        P("group"),
        P(None, ("group", "node"), None),
    )
    out_specs = (P(("group", "node"), None, "head", None), P(("group", "node"), None, "head", None))
    return jax.shard_map(
        functools.partial(local, 2),
        mesh=mesh,
        in_specs=in_specs,
        out_specs=out_specs,
        check_vma=False,
    )
```

time: 601 us -> 358 us (0.60); the launches traced: 591 us -> 357 us
  matrix products: 147 us -> 0 us
  Pallas kernels: 0 us -> 119 us
  other arithmetic: 111 us -> 5.82 us
  local copies, waits for them, and re-layouts: 72.9 us -> 15 us
  waiting for transfers between devices: 238 us -> 189 us
  starting transfers between devices: 21.5 us -> 27.9 us
    all_to_all x4, waiting for transfers between devices: 238 us -> 75.4 us  [exchange(): return lax.all_to_all(rows, 'node', split_axis=0, concat_axis=0, tiled=True)]
    dot_general x16 -> x0, matrix products: 147 us -> none  [the longest x8 79.2 us: one_head(): jnp.einsum('gtd,sd->gts', query_head, key_head, preferred_element_type=jn...]
    pallas_call x0 -> x9, Pallas kernels: none -> 119 us  [the longest x1 42.6 us: attend_second(): pl.pallas_call(functools.partial(second_kernel, chunk_count, source_count...]
    ppermute x0 -> x6, waiting for transfers between devices: none -> 113 us  [local(): arrived.append(lax.ppermute(packed[far], 'node', pairs))]
    reduce_sum x13 -> x1, other arithmetic: 86.2 us -> 0.14 us  [local_blocks(): jnp.sum(jnp.where(selected, (paths % per_owner)[:, :, None], 0), axis=1)]
    gather x8 -> x0, local copies, waits for them, and re-layouts: 47.1 us -> none  [outgoing(): return (cache_keys[block_index], cache_values[block_index])]
    transpose x6 -> x4, other arithmetic: 12.7 us -> 1.69 us  [the longest x1 0.77 us: local(): jnp.moveaxis(key_rot_two, 1, 0)]
    ppermute x0 -> x6, starting transfers between devices: none -> 8.55 us  [local(): arrived.append(lax.ppermute(packed[far], 'node', pairs))]
  transfers between devices with their start and end apart: 4 -> 10, of which waited for: 3 -> 5; matrix products, arithmetic and copies ran while one was open for 30% -> 3% of each run, Pallas kernels for 0% -> 32%
where the time goes in v1:
time: 358 us; the launch traced here: 357 us
  waiting for transfers between devices  189 us (53%)
  Pallas kernels  119 us (33%)
  starting transfers between devices  27.9 us (8%)
  local copies, waits for them, and re-layouts  15 us (4%)
  other arithmetic  5.82 us (2%)
    ppermute x6, waiting for transfers between devices, local(): arrived.append(lax.ppermute(packed[far], 'node', pairs))  113 us
    all_to_all x4, waiting for transfers between devices, exchange(): return lax.all_to_all(rows, 'node', split_axis=0, concat_axis=0, tiled=True)  75.4 us
    pallas_call x1, Pallas kernels, attend_second(): pl.pallas_call(functools.partial(second_kernel, chunk_count, source_count...  42.6 us
    pallas_call x2, Pallas kernels, attend_first(): pl.pallas_call(functools.partial(first_kernel, len(sources), part_rows, s...  37.1 us
    all_to_all x4, starting transfers between devices, exchange(): return lax.all_to_all(rows, 'node', split_axis=0, concat_axis=0, tiled=True)  19.4 us
    pallas_call x2, Pallas kernels, attend_own(): pl.pallas_call(functools.partial(own_kernel, row_count // token_count, sc...  15.8 us
    pallas_call x2, Pallas kernels, pack(): pl.pallas_call(functools.partial(pack_kernel, per_peer, head_count, token...  14 us
    pallas_call x2, Pallas kernels, merge(): pl.pallas_call(functools.partial(merge_kernel, head_count, group_size), g...  9.43 us
  transfers between devices with their start and end apart: 10, of which 5 were waited for; matrix products, arithmetic and copies ran while one was open for 3% of the time, Pallas kernels for 32%

profile of v1, /device:TPU:0, one launch (start us, length us, event | category | flops | bytes accessed | tf_op | source)
XLA Modules:
  0.0 357.2 jit_solution(14127715369252903561)
XLA Ops:
  0.6 0.7 convert_bitcast_fusion
  1.3 1.9 copy.64
  3.3 0.2 bitcast_convert_fusion
  3.5 2.0 copy.54
  5.5 0.2 bitcast_convert_fusion.1
  5.7 0.3 multiply_cosine_fusion
  6.0 0.6 subtract_convert_fusion
  6.7 0.7 copy.65
  7.4 1.7 tile.24
  9.1 7.4 %all-to-all-start.2 = ((bf16[8,1024,128]{2,1,0:T(8,128)(2,1)}), bf16[8,1024,128]{2,1,0:T(8,128)(2,1)}, u32[]{:S(2)}, u32[]{:S(2)}) async-start(bf16[8,1024,128]{2,1,0:T(8,128)(2,1)} %bitcast.27.query_ref), calls=%async_computation.2 | async-start | bytes 4194304 | tf_op jit(solution)/shard_map/all_to_all | solution.py:483
  16.5 0.2 reduce_window_sum.11
  17.0 0.7 reshape.174.index_ref
  17.7 6.8 %pack_rows.3 = (bf16[4096,128]{1,0:T(8,128)(2,1)}, bf16[4096,128]{1,0:T(8,128)(2,1)}, bf16[4096,128]{1,0:T(8,128)(2,1)}, bf16[4096,128]{1,0:T(8,128)(2,1)}) custom-call(s32[16]{0:T(128)} %reshape.174.index_ref, s32[1]{0:T(128)} %bitcast.8.head_ref, bf16[32,512,128]{2,1,0:T(8,128)(2,1)} %bitcast.49, bf16[32,512,128]{2,1,0:T(8,128)(2,1)} %bitcast.50, ...), custom_call_target="tpu_custom_call" | custom-call | bytes 8388608 | tf_op jit(solution)/shard_map/pack_rows/pallas_call | solution.py:97
  24.5 1.8 collective-permute-start.3
  26.5 0.7 copy.55
  27.2 37.7 %all-to-all-done.2.refs_0_ = bf16[8,1024,128]{2,1,0:T(8,128)(2,1)} async-done(((bf16[8,1024,128]{2,1,0:T(8,128)(2,1)}), bf16[8,1024,128]{2,1,0:T(8,128)(2,1)}, u32[]{:S(2)}, u32[]{:S(2)}) %all-to-all-start.2) | async-done | bytes 2097184 | tf_op jit(solution)/shard_map/all_to_all | solution.py:483
  64.9 1.6 tile.21
  66.5 3.8 %all-to-all-start = ((bf16[8,1024,128]{2,1,0:T(8,128)(2,1)}), bf16[8,1024,128]{2,1,0:T(8,128)(2,1)S(1)}, u32[]{:S(2)}, u32[]{:S(2)}) async-start(bf16[8,1024,128]{2,1,0:T(8,128)(2,1)} %bitcast.7.query_ref), calls=%async_computation | async-start | bytes 4194304 | tf_op jit(solution)/shard_map/all_to_all | solution.py:483
  70.6 0.1 subtract_convert_fusion.3
  71.0 0.7 reshape.171.index_ref
  71.7 0.8 pad_maximum_fusion.refs_8_
  72.5 7.1 %pack_rows.2 = (bf16[4352,128]{1,0:T(8,128)(2,1)}, bf16[4352,128]{1,0:T(8,128)(2,1)}, bf16[4352,128]{1,0:T(8,128)(2,1)}, bf16[4352,128]{1,0:T(8,128)(2,1)}) custom-call(s32[16]{0:T(128)} %reshape.171.index_ref, s32[1]{0:T(128)} %bitcast.8.head_ref, bf16[32,512,128]{2,1,0:T(8,128)(2,1)} %bitcast.53, bf16[32,512,128]{2,1,0:T(8,128)(2,1)} %bitcast.54, ...), custom_call_target="tpu_custom_call" | custom-call | bytes 8912896 | tf_op jit(solution)/shard_map/pack_rows/pallas_call | solution.py:97
  79.6 1.8 collective-permute-start
  81.4 1.5 collective-permute-start.1
  82.9 0.2 collective-permute-start.2
  83.1 1.9 collective-permute-start.4
  85.0 1.3 collective-permute-start.5
  86.3 0.7 pad_add_fusion.group_ref
  87.0 91.2 %collective-permute-done.4.refs_2_.refs_3_ = bf16[4096,128]{1,0:T(8,128)(2,1)} collective-permute-done((bf16[4096,128]{1,0:T(8,128)(2,1)}, bf16[4096,128]{1,0:T(8,128)(2,1)}, u32[]{:S(2)}, u32[]{:S(2)}) %collective-permute-start.4) | collective-permute-done | bytes 1048608 | tf_op jit(solution)/shard_map/ppermute | solution.py:507
  178.2 22.1 %collective-permute-done.5.refs_3_.refs_4_ = bf16[4096,128]{1,0:T(8,128)(2,1)} collective-permute-done((bf16[4096,128]{1,0:T(8,128)(2,1)}, bf16[4096,128]{1,0:T(8,128)(2,1)}, u32[]{:S(2)}, u32[]{:S(2)}) %collective-permute-start.5) | collective-permute-done | bytes 1048608 | tf_op jit(solution)/shard_map/ppermute | solution.py:507
  200.3 42.6 %attend_second.1 = bf16[8,1056,128]{2,1,0:T(8,128)(2,1)} custom-call(s32[8]{0:T(128)} %parent_ref.1, s32[2]{0:T(128)} %pad_add_fusion.group_ref, bf16[8,1024,128]{2,1,0:T(8,128)(2,1)} %all-to-all-done.2.refs_0_, bf16[4096,128]{1,0:T(8,128)(2,1)} %get-tuple-element.14.refs_0_.refs_1_, bf16[4096,128]{1,0:T(8,128)(2,1)} %collective-permute-done.3.refs_1_.refs_2_, ...), custom_call_target="tpu_custom_call" | custom-call | flops 18253611008 | bytes 13107200 | tf_op jit(solution)/shard_map/attend_second/pallas_call | solution.py:309
  242.9 1.4 copy-done.1
  244.3 3.8 %all-to-all-start.3 = ((bf16[8,1056,128]{2,1,0:T(8,128)(2,1)}), bf16[8,1056,128]{2,1,0:T(8,128)(2,1)S(1)}, u32[]{:S(2)}, u32[]{:S(2)}) async-start(bf16[8,1056,128]{2,1,0:T(8,128)(2,1)} %attend_second.1), calls=%async_computation.3 | async-start | bytes 4325376 | tf_op jit(solution)/shard_map/all_to_all | solution.py:483
  248.1 18.5 %attend_first.2.refs_4_ = bf16[8,1056,128]{2,1,0:T(8,128)(2,1)} custom-call(bf16[8,1024,128]{2,1,0:T(8,128)(2,1)} %copy-done.1, bf16[4096,128]{1,0:T(8,128)(2,1)} %get-tuple-element.14.refs_0_.refs_1_, bf16[4096,128]{1,0:T(8,128)(2,1)} %collective-permute-done.3.refs_1_.refs_2_, bf16[4096,128]{1,0:T(8,128)(2,1)} %collective-permute-done.4.refs_2_.refs_3_, ...), custom_call_target="tpu_custom_call" | custom-call | flops 8589934592 | bytes 6291456 | tf_op jit(solution)/shard_map/attend_first/pallas_call | solution.py:213
  266.6 18.6 %attend_first.3 = bf16[8,1056,128]{2,1,0:T(8,128)(2,1)} custom-call(bf16[8,1024,128]{2,1,0:T(8,128)(2,1)} %copy-done.1, bf16[4352,128]{1,0:T(8,128)(2,1)} %get-tuple-element.10.refs_0_.refs_5_, bf16[4352,128]{1,0:T(8,128)(2,1)} %collective-permute-done.refs_1_.refs_6_, ...), custom_call_target="tpu_custom_call", output_to_operand_aliasing={{}: (5, {})} | custom-call | flops 8589934592 | bytes 6291456 | tf_op jit(solution)/shard_map/attend_first/pallas_call | solution.py:213
  285.2 12.3 %all-to-all-done.3.part_ref.part_stat_ref = bf16[8,1056,128]{2,1,0:T(8,128)(2,1)S(1)} async-done(((bf16[8,1056,128]{2,1,0:T(8,128)(2,1)}), bf16[8,1056,128]{2,1,0:T(8,128)(2,1)S(1)}, u32[]{:S(2)}, u32[]{:S(2)}) %all-to-all-start.3) | async-done | bytes 2162720 | tf_op jit(solution)/shard_map/all_to_all | solution.py:483
  297.5 1.4 copy-done
  298.9 4.3 %all-to-all-start.1 = ((bf16[8,1056,128]{2,1,0:T(8,128)(2,1)}), bf16[8,1056,128]{2,1,0:T(8,128)(2,1)}, u32[]{:S(2)}, u32[]{:S(2)}) async-start(bf16[8,1056,128]{2,1,0:T(8,128)(2,1)} %attend_first.3), calls=%async_computation.1 | async-start | bytes 4325376 | tf_op jit(solution)/shard_map/all_to_all | solution.py:483
  303.5 0.7 copy.75
  304.1 0.7 copy.74
  304.8 0.1 subtract_convert_fusion.2
  305.0 0.8 maximum_bitcast_fusion.3.key_ref
  305.7 7.9 %attend_own.3.own_ref.own_stat_ref = bf16[4,1056,128]{2,1,0:T(8,128)(2,1)} custom-call(bf16[8,1024,128]{2,1,0:T(8,128)(2,1)} %bitcast.27.query_ref, bf16[4,128,128]{2,1,0:T(8,128)(2,1)} %maximum_bitcast_fusion.3.key_ref, bf16[4,128,128]{2,1,0:T(8,128)(2,1)} %bitcast.75), custom_call_target="tpu_custom_call" | custom-call | flops 536870912 | bytes 2359296 | tf_op jit(solution)/shard_map/attend_own/pallas_call | solution.py:363
  313.7 0.8 maximum_bitcast_fusion.2.key_ref
  314.4 7.9 %attend_own.2.own_ref.own_stat_ref = bf16[4,1056,128]{2,1,0:T(8,128)(2,1)} custom-call(bf16[8,1024,128]{2,1,0:T(8,128)(2,1)} %bitcast.7.query_ref, bf16[4,128,128]{2,1,0:T(8,128)(2,1)} %maximum_bitcast_fusion.2.key_ref, bf16[4,128,128]{2,1,0:T(8,128)(2,1)} %bitcast.74), custom_call_target="tpu_custom_call" | custom-call | flops 536870912 | bytes 2359296 | tf_op jit(solution)/shard_map/attend_own/pallas_call | solution.py:363
  322.3 4.7 %merge_parts.3 = bf16[1,128,32,128]{3,2,1,0:T(8,128)(2,1)} custom-call(bf16[8,1056,128]{2,1,0:T(8,128)(2,1)} %copy-done, bf16[4,1056,128]{2,1,0:T(8,128)(2,1)} %attend_own.3.own_ref.own_stat_ref, bf16[8,1056,128]{2,1,0:T(8,128)(2,1)} %copy-done, bf16[4,1056,128]{2,1,0:T(8,128)(2,1)} %attend_own.3.own_ref.own_stat_ref), custom_call_target="tpu_custom_call" | custom-call | flops 4194304 | bytes 4194304 | tf_op jit(solution)/shard_map/merge_parts/pallas_call | solution.py:428
  327.1 25.4 %all-to-all-done.1.part_ref.part_stat_ref = bf16[8,1056,128]{2,1,0:T(8,128)(2,1)} async-done(((bf16[8,1056,128]{2,1,0:T(8,128)(2,1)}), bf16[8,1056,128]{2,1,0:T(8,128)(2,1)}, u32[]{:S(2)}, u32[]{:S(2)}) %all-to-all-start.1) | async-done | bytes 2162720 | tf_op jit(solution)/shard_map/all_to_all | solution.py:483
  352.5 4.7 %merge_parts.2 = bf16[1,128,32,128]{3,2,1,0:T(8,128)(2,1)} custom-call(bf16[8,1056,128]{2,1,0:T(8,128)(2,1)} %all-to-all-done.1.part_ref.part_stat_ref, bf16[4,1056,128]{2,1,0:T(8,128)(2,1)} %attend_own.2.own_ref.own_stat_ref, bf16[8,1056,128]{2,1,0:T(8,128)(2,1)} %all-to-all-done.1.part_ref.part_stat_ref, bf16[4,1056,128]{2,1,0:T(8,128)(2,1)} %attend_own.2.own_ref.own_stat_ref), custom_call_target="tpu_custom_call" | custom-call | flops 4194304 | bytes 4194304 | tf_op jit(solution)/shard_map/merge_parts/pallas_call | solution.py:428
  (34 shorter events, 1.3 us)
Async XLA Ops:
  9.1 7.4 %copy-start.6 = (s32[8,32]{1,0:T(8,128)S(1)}, s32[8,32]{1,0:T(8,128)}, u32[]{:S(2)}) copy-start(s32[8,32]{1,0:T(8,128)} %param.19) | copy-start | bytes 3076
  9.1 55.8 %all-to-all-start.2 = ((bf16[8,1024,128]{2,1,0:T(8,128)(2,1)}), bf16[8,1024,128]{2,1,0:T(8,128)(2,1)}, u32[]{:S(2)}, u32[]{:S(2)}) async-start(bf16[8,1024,128]{2,1,0:T(8,128)(2,1)} %bitcast.27.query_ref), calls=%async_computation.2 | async-start | bytes 4194304 | tf_op jit(solution)/shard_map/all_to_all | solution.py:483
  24.5 60.5 %collective-permute-start.3 = (bf16[4096,128]{1,0:T(8,128)(2,1)}, bf16[4096,128]{1,0:T(8,128)(2,1)}, u32[]{:S(2)}, u32[]{:S(2)}) collective-permute-start(bf16[4096,128]{1,0:T(8,128)(2,1)} %get-tuple-element.15), channel_id=1, source_target_pairs={{0,2},{2,0},{4,6},{6,4},{8,10},{10,8},{12,14},{14,12},{1,3},{3,1},... | collective-permute-start | bytes 3145736 | tf_op jit(solution)/shard_map/ppermute | solution.py:507
  66.5 4.0 %copy-start.3 = (bf16[1,128,4,128]{3,2,1,0:T(4,128)(2,1)S(1)}, bf16[1,128,4,128]{3,2,1,0:T(4,128)(2,1)}, u32[]{:S(2)}) copy-start(bf16[1,128,4,128]{3,2,1,0:T(4,128)(2,1)} %param.12) | copy-start | bytes 393220
  66.5 176.4 %all-to-all-start = ((bf16[8,1024,128]{2,1,0:T(8,128)(2,1)}), bf16[8,1024,128]{2,1,0:T(8,128)(2,1)S(1)}, u32[]{:S(2)}, u32[]{:S(2)}) async-start(bf16[8,1024,128]{2,1,0:T(8,128)(2,1)} %bitcast.7.query_ref), calls=%async_computation | async-start | bytes 4194304 | tf_op jit(solution)/shard_map/all_to_all | solution.py:483
  79.6 120.7 %collective-permute-start = (bf16[4352,128]{1,0:T(8,128)(2,1)}, bf16[4352,128]{1,0:T(8,128)(2,1)}, u32[]{:S(2)}, u32[]{:S(2)}) collective-permute-start(bf16[4352,128]{1,0:T(8,128)(2,1)} %get-tuple-element.11), channel_id=1, source_target_pairs={{0,2},{2,0},{4,6},{6,4},{8,10},{10,8},{12,14},{14,12},{1,3},{3,1},... | collective-permute-start | bytes 3342344 | tf_op jit(solution)/shard_map/ppermute | solution.py:507
  81.4 119.0 %collective-permute-start.1 = (bf16[4352,128]{1,0:T(8,128)(2,1)}, bf16[4352,128]{1,0:T(8,128)(2,1)}, u32[]{:S(2)}, u32[]{:S(2)}) collective-permute-start(bf16[4352,128]{1,0:T(8,128)(2,1)} %get-tuple-element.12), channel_id=1, source_target_pairs={{0,4},{2,6},{4,0},{6,2},{8,12},{10,14},{12,8},{14,10},{1,5},{3,7},... | collective-permute-start | bytes 3342344 | tf_op jit(solution)/shard_map/ppermute | solution.py:507
  82.9 117.4 %collective-permute-start.2 = (bf16[4352,128]{1,0:T(8,128)(2,1)}, bf16[4352,128]{1,0:T(8,128)(2,1)}, u32[]{:S(2)}, u32[]{:S(2)}) collective-permute-start(bf16[4352,128]{1,0:T(8,128)(2,1)} %get-tuple-element.13), channel_id=1, source_target_pairs={{0,6},{2,4},{4,2},{6,0},{8,14},{10,12},{12,10},{14,8},{1,7},{3,5},... | collective-permute-start | bytes 3342344 | tf_op jit(solution)/shard_map/ppermute | solution.py:507
  83.1 95.1 %collective-permute-start.4 = (bf16[4096,128]{1,0:T(8,128)(2,1)}, bf16[4096,128]{1,0:T(8,128)(2,1)}, u32[]{:S(2)}, u32[]{:S(2)}) collective-permute-start(bf16[4096,128]{1,0:T(8,128)(2,1)} %get-tuple-element.16), channel_id=1, source_target_pairs={{0,4},{2,6},{4,0},{6,2},{8,12},{10,14},{12,8},{14,10},{1,5},{3,7},... | collective-permute-start | bytes 3145736 | tf_op jit(solution)/shard_map/ppermute | solution.py:507
  85.0 115.3 %collective-permute-start.5 = (bf16[4096,128]{1,0:T(8,128)(2,1)}, bf16[4096,128]{1,0:T(8,128)(2,1)}, u32[]{:S(2)}, u32[]{:S(2)}) collective-permute-start(bf16[4096,128]{1,0:T(8,128)(2,1)} %get-tuple-element.17), channel_id=1, source_target_pairs={{0,6},{2,4},{4,2},{6,0},{8,14},{10,12},{12,10},{14,8},{1,7},{3,5},... | collective-permute-start | bytes 3145736 | tf_op jit(solution)/shard_map/ppermute | solution.py:507
  242.9 1.4 copy-start.1
  244.3 53.2 %all-to-all-start.3 = ((bf16[8,1056,128]{2,1,0:T(8,128)(2,1)}), bf16[8,1056,128]{2,1,0:T(8,128)(2,1)S(1)}, u32[]{:S(2)}, u32[]{:S(2)}) async-start(bf16[8,1056,128]{2,1,0:T(8,128)(2,1)} %attend_second.1), calls=%async_computation.3 | async-start | bytes 4325376 | tf_op jit(solution)/shard_map/all_to_all | solution.py:483
  285.2 18.2 %copy-start.2 = (bf16[1,128,4,128]{3,2,1,0:T(4,128)(2,1)S(1)}, bf16[1,128,4,128]{3,2,1,0:T(4,128)(2,1)}, u32[]{:S(2)}) copy-start(bf16[1,128,4,128]{3,2,1,0:T(4,128)(2,1)} %param.13) | copy-start | bytes 393220
  285.2 18.9 %copy-start.5 = (bf16[1,128,4,128]{3,2,1,0:T(4,128)(2,1)S(1)}, bf16[1,128,4,128]{3,2,1,0:T(4,128)(2,1)}, u32[]{:S(2)}) copy-start(bf16[1,128,4,128]{3,2,1,0:T(4,128)(2,1)} %param.16) | copy-start | bytes 393220
  285.2 19.6 %copy-start.4 = (bf16[1,128,4,128]{3,2,1,0:T(4,128)(2,1)S(1)}, bf16[1,128,4,128]{3,2,1,0:T(4,128)(2,1)}, u32[]{:S(2)}) copy-start(bf16[1,128,4,128]{3,2,1,0:T(4,128)(2,1)} %param.15) | copy-start | bytes 393220
  297.5 1.4 copy-start
  298.9 53.6 %all-to-all-start.1 = ((bf16[8,1056,128]{2,1,0:T(8,128)(2,1)}), bf16[8,1056,128]{2,1,0:T(8,128)(2,1)}, u32[]{:S(2)}, u32[]{:S(2)}) async-start(bf16[8,1056,128]{2,1,0:T(8,128)(2,1)} %attend_first.3), calls=%async_computation.1 | async-start | bytes 4325376 | tf_op jit(solution)/shard_map/all_to_all | solution.py:483

commit v2 on v1

--- a/solution.py
+++ b/solution.py
@@ -14,24 +14,60 @@
 vmem_bytes = 56 * 1024 * 1024
 
 
-def rotary(vector, position_row):
-    head_width = vector.shape[-1]
+def rotary_tables(positions, head_width):
     half_width = head_width // 2
     frequency = rope_theta ** (-(jnp.arange(half_width, dtype=jnp.float32) * 2.0) / head_width)
-    angles = position_row.astype(jnp.float32)[:, None] * frequency[None, :]
-    cosine = jnp.cos(angles)[:, None, :]
-    sine_part = jnp.sin(angles)[:, None, :]
+    angles = positions.astype(jnp.float32)[..., None] * frequency
+    cosine = jnp.cos(angles)
+    sine_part = jnp.sin(angles)
+    return jnp.concatenate([cosine, cosine], -1), jnp.concatenate([-sine_part, sine_part], -1)
+
+
+def rotary(vector, cosine, signed_sine):
     widened = vector.astype(jnp.float32)
-    first_half = widened[..., :half_width]
-    second_half = widened[..., half_width:]
-    turned = jnp.concatenate(
-        [
-            first_half * cosine - second_half * sine_part,
-            second_half * cosine + first_half * sine_part,
-        ],
-        -1,
-    )
+    swapped = jnp.roll(widened, widened.shape[-1] // 2, axis=-1)
+    turned = widened * cosine[:, None, :] + swapped * signed_sine[:, None, :]
     return turned.astype(jnp.bfloat16)
+
+
+def turn_kernel(head_count, copies, first_ref, second_ref, cosine_ref, sine_ref, out_ref):
+    token_tile, query_heads, width = first_ref.shape[1:]
+    group_size = query_heads // head_count
+    rows = token_tile * group_size
+    for depth, query_ref in enumerate((first_ref, second_ref)):
+        widened = query_ref[0].astype(jnp.float32)
+        swapped = pltpu.roll(widened.reshape(token_tile * query_heads, width), width // 2, 1)
+        swapped = swapped.reshape(token_tile, query_heads, width)
+        turned = widened * cosine_ref[depth][:, None, :] + swapped * sine_ref[depth][:, None, :]
+        for head in range(head_count):
+            turned_head = turned[:, head * group_size : (head + 1) * group_size, :]
+            turned_head = turned_head.reshape(rows, width).astype(jnp.bfloat16)
+            for copy in range(copies):
+                out_ref[copy * head_count + head, depth] = turned_head
+
+
+def turn_queries(queries_one, queries_two, cosine, sine_part, head_count, copies):
+    _, token_count, query_heads, width = queries_one.shape
+    token_tile = 32
+    rows = token_tile * query_heads // head_count
+    query_spec = pl.BlockSpec((1, token_tile, query_heads, width), lambda step: (0, step, 0, 0))
+    table_spec = pl.BlockSpec((2, token_tile, width), lambda step: (0, step, 0))
+    return pl.pallas_call(
+        functools.partial(turn_kernel, head_count, copies),
+        grid=(token_count // token_tile,),
+        in_specs=[query_spec, query_spec, table_spec, table_spec],
+        out_specs=pl.BlockSpec(
+            (head_count * copies, 2, rows, width), lambda step: (0, 0, step, 0)
+        ),
+        out_shape=jax.ShapeDtypeStruct(
+            (head_count * copies, 2, token_count * query_heads // head_count, width), jnp.bfloat16
+        ),
+        compiler_params=pltpu.CompilerParams(vmem_limit_bytes=vmem_bytes),
+        cost_estimate=pl.CostEstimate(
+            flops=8 * queries_one.size, bytes_accessed=12 * queries_one.size, transcendentals=0
+        ),
+        name="turn_queries",
+    )(queries_one, queries_two, cosine, sine_part)
 
 
 def local_blocks(paths, here_index, per_owner, per_peer):
@@ -50,8 +86,8 @@
     refs = refs[2 * per_peer :]
     new_refs = ()
     if with_new:
-        new_refs, refs = refs[:2], refs[2:]
-    out_refs, wide = refs[:head_count], refs[head_count]
+        new_refs = refs[:2]
+    out_refs, wide = refs[-1 - head_count : -1], refs[-1]
     step = pl.program_id(0)
     mine = head_ref[0]
     span_rows = 2 * per_peer * token_count
@@ -76,7 +112,7 @@
                 spread(source[...], pl.multiple_of(base + which * token_count, token_count))
 
 
-def pack(cache_keys, cache_values, block_index, head_index, new_rows, per_peer):
+def pack(cache_keys, cache_values, block_index, head_index, new_rows, per_peer, before=()):
     block_count, token_count, head_count, width = cache_keys.shape
     path_count = block_index.shape[0]
     flat_keys = cache_keys.reshape(block_count, token_count * head_count, width)
@@ -99,7 +135,10 @@
         grid_spec=pltpu.PrefetchScalarGridSpec(
             num_scalar_prefetch=2,
             grid=(path_count,),
-            in_specs=cache_specs + cache_specs + [new_spec] * len(new_rows),
+            in_specs=cache_specs
+            + cache_specs
+            + [new_spec] * len(new_rows)
+            + [pl.BlockSpec(memory_space=pl.ANY)] * len(before),
             out_specs=[pl.BlockSpec((out_rows, width), lambda step, index, head: (0, 0))]
             * head_count,
             scratch_shapes=[pltpu.VMEM((token_count * head_count, width), jnp.float32)],
@@ -110,7 +149,7 @@
             flops=0, bytes_accessed=4 * head_count * out_rows * width, transcendentals=0
         ),
         name="pack_rows",
-    )(block_index.reshape(-1), head_index, *operands)
+    )(block_index.reshape(-1), head_index, *operands, *before)
 
 
 def eye(size):
@@ -196,30 +235,34 @@
     return keys, values
 
 
-def first_kernel(source_count, part_rows, score_scale, has_base, query_ref, *refs):
+def first_kernel(source_count, part_rows, score_scale, query_ref, *refs):
     source_refs = refs[:source_count]
-    out_ref, level_ref = refs[source_count + has_base :]
+    out_ref, mark_ref, level_ref = refs[-3:]
+    mark_ref[...] = jnp.zeros_like(mark_ref)
     keys, values = part_readers(source_refs, part_rows)
     attend_task(query_ref, out_ref, level_ref, keys, values, None, score_scale)
 
 
-def attend_first(queries, sources, base, first_path, path_count, part_rows, score_scale):
-    span_count, row_count, width = queries.shape
+def attend_first(queries, sources, base, first_path, path_count, part_rows, score_scale, before):
+    span_count, _, row_count, width = queries.shape
     span_rows = 2 * part_rows
     out_shape = jax.ShapeDtypeStruct((span_count, row_count + stat_rows, width), jnp.bfloat16)
     has_base = int(base is not None)
-    operands = [queries, *sources] + ([base] if has_base else [])
+    operands = [queries, *sources, *before] + ([base] if has_base else [])
     keys = len(sources) * part_rows
     return pl.pallas_call(
-        functools.partial(first_kernel, len(sources), part_rows, score_scale, has_base),
+        functools.partial(first_kernel, len(sources), part_rows, score_scale),
         grid=(path_count,),
-        in_specs=[pl.BlockSpec((1, row_count, width), lambda step: (first_path + step, 0, 0))]
+        in_specs=[
+            pl.BlockSpec((1, None, row_count, width), lambda step: (first_path + step, 0, 0, 0))
+        ]
         + [pl.BlockSpec((span_rows, width), lambda step: (step, 0))] * len(sources)
-        + [pl.BlockSpec(memory_space=pl.ANY)] * has_base,
-        out_specs=pl.BlockSpec(
-            (1, row_count + stat_rows, width), lambda step: (first_path + step, 0, 0)
-        ),
-        out_shape=out_shape,
+        + [pl.BlockSpec(memory_space=pl.ANY)] * (len(before) + has_base),
+        out_specs=[
+            pl.BlockSpec((1, row_count + stat_rows, width), lambda step: (first_path + step, 0, 0)),
+            pl.BlockSpec((8, width), lambda step: (0, 0)),
+        ],
+        out_shape=[out_shape, jax.ShapeDtypeStruct((8, width), jnp.float32)],
         scratch_shapes=[pltpu.VMEM((row_count // width, width), jnp.float32)],
         input_output_aliases={len(operands) - 1: 0} if has_base else {},
         compiler_params=pltpu.CompilerParams(vmem_limit_bytes=vmem_bytes),
@@ -237,7 +280,7 @@
 ):
     query_ref = refs[0]
     source_refs = refs[1 : 1 + chunk_count * source_count]
-    out_ref, level_ref, held, fresh, semaphores = refs[1 + chunk_count * source_count :]
+    out_ref, level_ref, held, fresh, semaphores = refs[-5:]
     span_rows = 2 * part_rows
     token_count = fresh.shape[1] // 2
     step = pl.program_id(0)
@@ -297,8 +340,10 @@
     attend_task(query_ref, out_ref, level_ref, keys, values, mask_of, score_scale)
 
 
-def attend_second(queries, chunks, parents, group_index, chunk_paths, part_rows, score_scale):
-    span_count, row_count, width = queries.shape
+def attend_second(
+    queries, chunks, parents, group_index, chunk_paths, part_rows, score_scale, before
+):
+    span_count, _, row_count, width = queries.shape
     source_count = len(chunks[0])
     chunk_count = len(chunks)
     span_rows = 2 * part_rows
@@ -313,8 +358,12 @@
         grid_spec=pltpu.PrefetchScalarGridSpec(
             num_scalar_prefetch=2,
             grid=(span_count,),
-            in_specs=[pl.BlockSpec((1, row_count, width), lambda step, parent, group: (step, 0, 0))]
-            + [pl.BlockSpec(memory_space=pl.ANY)] * len(operands),
+            in_specs=[
+                pl.BlockSpec(
+                    (1, None, row_count, width), lambda step, parent, group: (step, 1, 0, 0)
+                )
+            ]
+            + [pl.BlockSpec(memory_space=pl.ANY)] * (len(operands) + len(before)),
             out_specs=pl.BlockSpec(
                 (1, row_count + stat_rows, width), lambda step, parent, group: (step, 0, 0)
             ),
@@ -335,7 +384,7 @@
             transcendentals=span_count * row_count * keys,
         ),
         name="attend_second",
-    )(parents, group_index, queries, *operands)
+    )(parents, group_index, queries, *operands, *before)
 
 
 def own_kernel(group_size, score_scale, query_ref, key_ref, value_ref, out_ref, level_ref):
@@ -357,14 +406,14 @@
     )
 
 
-def attend_own(queries, keys, values, score_scale):
+def attend_own(queries, depth, keys, values, score_scale):
     head_count, token_count, width = keys.shape
-    row_count = queries.shape[1]
+    row_count = queries.shape[2]
     return pl.pallas_call(
         functools.partial(own_kernel, row_count // token_count, score_scale),
         grid=(head_count,),
         in_specs=[
-            pl.BlockSpec((1, row_count, width), lambda step: (step, 0, 0)),
+            pl.BlockSpec((1, None, row_count, width), lambda step: (step, depth, 0, 0)),
             pl.BlockSpec((1, token_count, width), lambda step: (step, 0, 0)),
             pl.BlockSpec((1, token_count, width), lambda step: (step, 0, 0)),
         ],
@@ -474,18 +523,14 @@
     my_head = here_index % head_count
     my_group = here_index // head_count
 
-    def by_head(rotated):
-        split = rotated.reshape(token_count, head_count, group_size, width)
-        rows = jnp.moveaxis(split, 1, 0).reshape(head_count, token_count * group_size, width)
-        return jnp.tile(rows, (copies, 1, 1))
-
     def exchange(rows):
         return lax.all_to_all(rows, "node", split_axis=0, concat_axis=0, tiled=True)
 
-    send_one = by_head(rotary(queries_one[0], positions[0, 0]))
-    got_one = exchange(send_one)
-    key_rot_one = rotary(keys_one[0], positions[0, 0])
-    key_rot_two = rotary(keys_two[0], positions[1, 0])
+    cosine, sine_part = rotary_tables(positions[:, 0], width)
+    send = turn_queries(queries_one, queries_two, cosine, sine_part, head_count, copies)
+    got = exchange(send)
+    key_rot_one = rotary(keys_one[0], cosine[0], sine_part[0])
+    key_rot_two = rotary(keys_two[0], cosine[1], sine_part[1])
 
     block_index = local_blocks(paths, here_index, block_count, per_peer)
     chunk_paths = peer_count // chunk_count
@@ -500,6 +545,7 @@
             my_head[None],
             (key_rot_one, values_one[0]) if last else (),
             per_peer,
+            (send,) if chunk == 0 else (packed[0],),
         )
         arrived = [packed[0]]
         for far in range(1, head_count):
@@ -507,36 +553,35 @@
             arrived.append(lax.ppermute(packed[far], "node", pairs))
         chunks.append(arrived)
 
-    send_two = by_head(rotary(queries_two[0], positions[1, 0]))
-    got_two = exchange(send_two)
-
     own_one = attend_own(
-        send_one, jnp.moveaxis(key_rot_one, 1, 0), jnp.moveaxis(values_one[0], 1, 0), score_scale
+        send, 0, jnp.moveaxis(key_rot_one, 1, 0), jnp.moveaxis(values_one[0], 1, 0), score_scale
     )
     own_two = attend_own(
-        send_two, jnp.moveaxis(key_rot_two, 1, 0), jnp.moveaxis(values_two[0], 1, 0), score_scale
+        send, 1, jnp.moveaxis(key_rot_two, 1, 0), jnp.moveaxis(values_two[0], 1, 0), score_scale
     )
 
     partial_one = None
     for chunk in range(chunk_count):
-        partial_one = attend_first(
-            got_one,
+        partial_one, mark = attend_first(
+            got,
             chunks[chunk],
             partial_one,
             chunk * chunk_paths,
             chunk_paths,
             part_rows,
             score_scale,
+            (own_one, own_two) if chunk == 0 else (),
         )
     parts_one = exchange(partial_one)
     partial_two = attend_second(
-        got_two,
+        got,
         chunks,
         parents,
         jnp.stack([my_group, my_head]),
         chunk_paths,
         part_rows,
         score_scale,
+        (mark,),
     )
     parts_two = exchange(partial_two)
     return merge(parts_one, own_one, token_count), merge(parts_two, own_two, token_count)

time: 358 us -> 309 us (0.86)
  waiting for transfers between devices: 189 us -> 151 us
  local copies, waits for them, and re-layouts: 15 us -> 3.75 us
  Pallas kernels: 119 us -> 124 us
  starting transfers between devices: 27.9 us -> 23.5 us
    all_to_all x4 -> x3, waiting for transfers between devices: 75.4 us -> 50.7 us  [exchange(): return lax.all_to_all(rows, 'node', split_axis=0, concat_axis=0, tiled=True)]
    ppermute x6, waiting for transfers between devices: 113 us -> 100 us  [local(): arrived.append(lax.ppermute(packed[far], 'node', pairs))]
    unnamed x18 -> x16, local copies, waits for them, and re-layouts: 8.02 us -> 1.37 us
    pallas_call x0 -> x1, Pallas kernels: none -> 4.68 us  [turn_queries(): pl.pallas_call(functools.partial(turn_kernel, head_count, copies), grid=(...]
    all_to_all x4 -> x3, starting transfers between devices: 19.4 us -> 15.6 us  [exchange(): return lax.all_to_all(rows, 'node', split_axis=0, concat_axis=0, tiled=True)]
  transfers between devices with their start and end apart: 10 -> 9, of which waited for: 5 -> 7; matrix products, arithmetic and copies ran while one was open for 3% -> 2% of each run, Pallas kernels for 32% -> 31%
where the time goes in v2:
time: 309 us; the launch traced here: 308 us
  waiting for transfers between devices  151 us (49%)
  Pallas kernels  124 us (40%)
  starting transfers between devices  23.5 us (8%)
  other arithmetic  5.63 us (2%)
  local copies, waits for them, and re-layouts  3.75 us (1%)
    ppermute x6, waiting for transfers between devices, local(): arrived.append(lax.ppermute(packed[far], 'node', pairs))  100 us
    all_to_all x3, waiting for transfers between devices, exchange(): return lax.all_to_all(rows, 'node', split_axis=0, concat_axis=0, tiled=True)  50.7 us
    pallas_call x1, Pallas kernels, attend_second(): pl.pallas_call(functools.partial(second_kernel, chunk_count, source_count...  42.6 us
    pallas_call x2, Pallas kernels, attend_first(): pl.pallas_call(functools.partial(first_kernel, len(sources), part_rows, s...  37 us
    pallas_call x2, Pallas kernels, attend_own(): pl.pallas_call(functools.partial(own_kernel, row_count // token_count, sc...  15.9 us
    all_to_all x3, starting transfers between devices, exchange(): return lax.all_to_all(rows, 'node', split_axis=0, concat_axis=0, tiled=True)  15.6 us
    pallas_call x2, Pallas kernels, pack(): pl.pallas_call(functools.partial(pack_kernel, per_peer, head_count, token...  14 us
    pallas_call x2, Pallas kernels, merge(): pl.pallas_call(functools.partial(merge_kernel, head_count, group_size), g...  9.46 us
  transfers between devices with their start and end apart: 9, of which 7 were waited for; matrix products, arithmetic and copies ran while one was open for 2% of the time, Pallas kernels for 31%

profile of v2, /device:TPU:0, one launch (start us, length us, event | category | flops | bytes accessed | tf_op | source)
XLA Modules:
  0.0 308.4 jit_solution(3576630328068774187)
XLA Ops:
  0.6 0.7 convert_element_type.40
  1.3 0.5 fusion.17
  1.9 0.8 pad_maximum_fusion
  2.7 4.7 %turn_queries.1.refs_8_.query_ref = bf16[8,2,1024,128]{3,2,1,0:T(8,128)(2,1)} custom-call(bf16[1,128,32,128]{3,2,1,0:T(8,128)(2,1)} %first_ref.1, bf16[1,128,32,128]{3,2,1,0:T(8,128)(2,1)} %second_ref.1, f32[2,128,128]{2,1,0:T(8,128)} %get-tuple-element.41.cosine_ref, f32[2,128,128]{2,1,0:T(8,128)} %get-tuple-element.42.sine_ref), custom_call_target="tpu_custom_call" | custom-call | flops 4194304 | bytes 6291456 | tf_op jit(solution)/shard_map/turn_queries/pallas_call | solution.py:55
  7.4 7.4 %all-to-all-start = ((bf16[8,2,1024,128]{3,2,1,0:T(8,128)(2,1)}), bf16[8,2,1024,128]{3,2,1,0:T(8,128)(2,1)}, u32[]{:S(2)}, u32[]{:S(2)}) async-start(bf16[8,2,1024,128]{3,2,1,0:T(8,128)(2,1)} %turn_queries.1.refs_8_.query_ref), calls=%async_computation | async-start | bytes 8388608 | tf_op jit(solution)/shard_map/all_to_all | solution.py:527
  14.8 0.2 reduce_window_sum.11
  15.0 0.1 select_reduce_fusion
  15.2 0.1 fusion.26
  15.2 0.1 copy.34
  15.3 0.7 reshape.59.index_ref
  16.0 6.9 %pack_rows.2 = (bf16[4096,128]{1,0:T(8,128)(2,1)}, bf16[4096,128]{1,0:T(8,128)(2,1)}, bf16[4096,128]{1,0:T(8,128)(2,1)}, bf16[4096,128]{1,0:T(8,128)(2,1)}) custom-call(s32[16]{0:T(128)} %reshape.59.index_ref, s32[1]{0:T(128)} %bitcast.1.head_ref, bf16[32,512,128]{2,1,0:T(8,128)(2,1)} %bitcast.42, bf16[32,512,128]{2,1,0:T(8,128)(2,1)} %bitcast.43, ...), custom_call_target="tpu_custom_call" | custom-call | bytes 8388608 | tf_op jit(solution)/shard_map/pack_rows/pallas_call | solution.py:133
  22.9 2.1 collective-permute-start.3
  25.0 1.4 collective-permute-start.4
  26.4 0.2 collective-permute-start.5
  26.6 0.2 copy.29
  26.8 0.1 fusion.25
  26.9 0.2 copy.31
  27.1 0.2 copy.32
  27.3 0.1 fusion.11
  27.5 0.8 fusion.1.refs_8_
  28.3 0.1 copy.27
  28.4 0.6 reshape.56.index_ref
  29.0 7.1 %pack_rows.3 = (bf16[4352,128]{1,0:T(8,128)(2,1)}, bf16[4352,128]{1,0:T(8,128)(2,1)}, bf16[4352,128]{1,0:T(8,128)(2,1)}, bf16[4352,128]{1,0:T(8,128)(2,1)}) custom-call(s32[16]{0:T(128)} %reshape.56.index_ref, s32[1]{0:T(128)} %bitcast.1.head_ref, bf16[32,512,128]{2,1,0:T(8,128)(2,1)} %bitcast.46, bf16[32,512,128]{2,1,0:T(8,128)(2,1)} %bitcast.47, ...), custom_call_target="tpu_custom_call" | custom-call | bytes 8912896 | tf_op jit(solution)/shard_map/pack_rows/pallas_call | solution.py:133
  36.1 2.0 collective-permute-start
  38.1 1.3 collective-permute-start.1
  39.4 0.7 copy.50
  40.1 0.1 fusion.24
  40.2 0.8 fusion.6.key_ref
  41.1 45.1 %collective-permute-done.3.refs_1_.refs_2_ = bf16[4096,128]{1,0:T(8,128)(2,1)} collective-permute-done((bf16[4096,128]{1,0:T(8,128)(2,1)}, bf16[4096,128]{1,0:T(8,128)(2,1)}, u32[]{:S(2)}, u32[]{:S(2)}) %collective-permute-start.3) | collective-permute-done | bytes 1048608 | tf_op jit(solution)/shard_map/ppermute | solution.py:553
  86.1 1.0 collective-permute-start.2
  87.2 8.0 %attend_own.3.refs_5_.own_ref.own_stat_ref = bf16[4,1056,128]{2,1,0:T(8,128)(2,1)} custom-call(bf16[8,2,1024,128]{3,2,1,0:T(8,128)(2,1)} %turn_queries.1.refs_8_.query_ref, bf16[4,128,128]{2,1,0:T(8,128)(2,1)} %fusion.6.key_ref, bf16[4,128,128]{2,1,0:T(8,128)(2,1)} %bitcast.64), custom_call_target="tpu_custom_call" | custom-call | flops 536870912 | bytes 2359296 | tf_op jit(solution)/shard_map/attend_own/pallas_call | solution.py:412
  95.2 0.7 copy.51
  95.8 0.8 fusion.7.key_ref
  96.6 8.0 %attend_own.2.refs_4_.own_ref.own_stat_ref = bf16[4,1056,128]{2,1,0:T(8,128)(2,1)} custom-call(bf16[8,2,1024,128]{3,2,1,0:T(8,128)(2,1)} %turn_queries.1.refs_8_.query_ref, bf16[4,128,128]{2,1,0:T(8,128)(2,1)} %fusion.7.key_ref, bf16[4,128,128]{2,1,0:T(8,128)(2,1)} %bitcast.65), custom_call_target="tpu_custom_call" | custom-call | flops 536870912 | bytes 2359296 | tf_op jit(solution)/shard_map/attend_own/pallas_call | solution.py:412
  104.6 4.0 %collective-permute-done.4.refs_2_.refs_3_ = bf16[4096,128]{1,0:T(8,128)(2,1)} collective-permute-done((bf16[4096,128]{1,0:T(8,128)(2,1)}, bf16[4096,128]{1,0:T(8,128)(2,1)}, u32[]{:S(2)}, u32[]{:S(2)}) %collective-permute-start.4) | collective-permute-done | bytes 1048608 | tf_op jit(solution)/shard_map/ppermute | solution.py:553
  108.6 23.0 %collective-permute-done.5.refs_3_.refs_4_ = bf16[4096,128]{1,0:T(8,128)(2,1)} collective-permute-done((bf16[4096,128]{1,0:T(8,128)(2,1)}, bf16[4096,128]{1,0:T(8,128)(2,1)}, u32[]{:S(2)}, u32[]{:S(2)}) %collective-permute-start.5) | collective-permute-done | bytes 1048608 | tf_op jit(solution)/shard_map/ppermute | solution.py:553
  131.7 18.4 %attend_first.2 = (bf16[8,1056,128]{2,1,0:T(8,128)(2,1)}, f32[8,128]{1,0:T(8,128)}) custom-call(bf16[8,2,1024,128]{3,2,1,0:T(8,128)(2,1)} %all-to-all-done.query_ref.refs_0_, bf16[4096,128]{1,0:T(8,128)(2,1)} %get-tuple-element.13.refs_10_.refs_0_.refs_1_, bf16[4096,128]{1,0:T(8,128)(2,1)} %collective-permute-done.3.refs_1_.refs_2_, ...), custom_call_target="tpu_custom_call" | custom-call | flops 8589934592 | bytes 6291456 | tf_op jit(solution)/shard_map/attend_first/pallas_call | solution.py:253
  150.1 4.9 %collective-permute-done.1.refs_2_.refs_7_ = bf16[4352,128]{1,0:T(8,128)(2,1)} collective-permute-done((bf16[4352,128]{1,0:T(8,128)(2,1)}, bf16[4352,128]{1,0:T(8,128)(2,1)}, u32[]{:S(2)}, u32[]{:S(2)}) %collective-permute-start.1) | collective-permute-done | bytes 1114144 | tf_op jit(solution)/shard_map/ppermute | solution.py:553
  155.0 23.4 %collective-permute-done.2.refs_3_.refs_8_ = bf16[4352,128]{1,0:T(8,128)(2,1)} collective-permute-done((bf16[4352,128]{1,0:T(8,128)(2,1)}, bf16[4352,128]{1,0:T(8,128)(2,1)}, u32[]{:S(2)}, u32[]{:S(2)}) %collective-permute-start.2) | collective-permute-done | bytes 1114144 | tf_op jit(solution)/shard_map/ppermute | solution.py:553
  178.4 18.5 %attend_first.3 = (bf16[8,1056,128]{2,1,0:T(8,128)(2,1)}, f32[8,128]{1,0:T(8,128)}) custom-call(bf16[8,2,1024,128]{3,2,1,0:T(8,128)(2,1)} %all-to-all-done.query_ref.refs_0_, bf16[4352,128]{1,0:T(8,128)(2,1)} %get-tuple-element.14.refs_0_.refs_5_, bf16[4352,128]{1,0:T(8,128)(2,1)} %copy-done.6, ...), custom_call_target="tpu_custom_call", output_to_operand_aliasing={{0}: (5, {})} | custom-call | flops 8589934592 | bytes 6291456 | tf_op jit(solution)/shard_map/attend_first/pallas_call | solution.py:253
  196.9 3.8 %all-to-all-start.1 = ((bf16[8,1056,128]{2,1,0:T(8,128)(2,1)}), bf16[8,1056,128]{2,1,0:T(8,128)(2,1)S(1)}, u32[]{:S(2)}, u32[]{:S(2)}) async-start(bf16[8,1056,128]{2,1,0:T(8,128)(2,1)} %get-tuple-element.22), calls=%async_computation.1 | async-start | bytes 4325376 | tf_op jit(solution)/shard_map/all_to_all | solution.py:527
  200.7 0.6 pad_add_fusion.group_ref
  201.3 42.6 %attend_second.1 = bf16[8,1056,128]{2,1,0:T(8,128)(2,1)} custom-call(s32[8]{0:T(128)} %parent_ref.1, s32[2]{0:T(128)} %pad_add_fusion.group_ref, bf16[8,2,1024,128]{3,2,1,0:T(8,128)(2,1)} %all-to-all-done.query_ref.refs_0_, bf16[4096,128]{1,0:T(8,128)(2,1)} %get-tuple-element.13.refs_10_.refs_0_.refs_1_, ...), custom_call_target="tpu_custom_call" | custom-call | flops 18253611008 | bytes 13107200 | tf_op jit(solution)/shard_map/attend_second/pallas_call | solution.py:354
  243.9 6.2 %all-to-all-done.1.part_ref.part_stat_ref = bf16[8,1056,128]{2,1,0:T(8,128)(2,1)S(1)} async-done(((bf16[8,1056,128]{2,1,0:T(8,128)(2,1)}), bf16[8,1056,128]{2,1,0:T(8,128)(2,1)S(1)}, u32[]{:S(2)}, u32[]{:S(2)}) %all-to-all-start.1) | async-done | bytes 2162720 | tf_op jit(solution)/shard_map/all_to_all | solution.py:527
  250.1 4.4 %all-to-all-start.2 = ((bf16[8,1056,128]{2,1,0:T(8,128)(2,1)}), bf16[8,1056,128]{2,1,0:T(8,128)(2,1)}, u32[]{:S(2)}, u32[]{:S(2)}) async-start(bf16[8,1056,128]{2,1,0:T(8,128)(2,1)} %attend_second.1), calls=%async_computation.2 | async-start | bytes 4325376 | tf_op jit(solution)/shard_map/all_to_all | solution.py:527
  254.4 4.7 %merge_parts.2 = bf16[1,128,32,128]{3,2,1,0:T(8,128)(2,1)} custom-call(bf16[8,1056,128]{2,1,0:T(8,128)(2,1)} %copy-done, bf16[4,1056,128]{2,1,0:T(8,128)(2,1)} %attend_own.2.refs_4_.own_ref.own_stat_ref, bf16[8,1056,128]{2,1,0:T(8,128)(2,1)} %copy-done, bf16[4,1056,128]{2,1,0:T(8,128)(2,1)} %attend_own.2.refs_4_.own_ref.own_stat_ref), custom_call_target="tpu_custom_call" | custom-call | flops 4194304 | bytes 4194304 | tf_op jit(solution)/shard_map/merge_parts/pallas_call | solution.py:477
  259.2 44.5 %all-to-all-done.2.part_ref.part_stat_ref = bf16[8,1056,128]{2,1,0:T(8,128)(2,1)} async-done(((bf16[8,1056,128]{2,1,0:T(8,128)(2,1)}), bf16[8,1056,128]{2,1,0:T(8,128)(2,1)}, u32[]{:S(2)}, u32[]{:S(2)}) %all-to-all-start.2) | async-done | bytes 2162720 | tf_op jit(solution)/shard_map/all_to_all | solution.py:527
  303.7 4.7 %merge_parts.3 = bf16[1,128,32,128]{3,2,1,0:T(8,128)(2,1)} custom-call(bf16[8,1056,128]{2,1,0:T(8,128)(2,1)} %all-to-all-done.2.part_ref.part_stat_ref, bf16[4,1056,128]{2,1,0:T(8,128)(2,1)} %attend_own.3.refs_5_.own_ref.own_stat_ref, bf16[8,1056,128]{2,1,0:T(8,128)(2,1)} %all-to-all-done.2.part_ref.part_stat_ref, ...), custom_call_target="tpu_custom_call" | custom-call | flops 4194304 | bytes 4194304 | tf_op jit(solution)/shard_map/merge_parts/pallas_call | solution.py:477
  (23 shorter events, 0.2 us)
Async XLA Ops:
  7.4 7.4 %copy-start.5 = (s32[8,32]{1,0:T(8,128)S(1)}, s32[8,32]{1,0:T(8,128)}, u32[]{:S(2)}) copy-start(s32[8,32]{1,0:T(8,128)} %param.19) | copy-start | bytes 3076
  7.4 124.3 %all-to-all-start = ((bf16[8,2,1024,128]{3,2,1,0:T(8,128)(2,1)}), bf16[8,2,1024,128]{3,2,1,0:T(8,128)(2,1)}, u32[]{:S(2)}, u32[]{:S(2)}) async-start(bf16[8,2,1024,128]{3,2,1,0:T(8,128)(2,1)} %turn_queries.1.refs_8_.query_ref), calls=%async_computation | async-start | bytes 8388608 | tf_op jit(solution)/shard_map/all_to_all | solution.py:527
  16.0 10.5 %copy-start.3 = (bf16[1,128,4,128]{3,2,1,0:T(4,128)(2,1)S(1)}, bf16[1,128,4,128]{3,2,1,0:T(4,128)(2,1)}, u32[]{:S(2)}) copy-start(bf16[1,128,4,128]{3,2,1,0:T(4,128)(2,1)} %param.12) | copy-start | bytes 393220
  22.9 63.2 %collective-permute-start.3 = (bf16[4096,128]{1,0:T(8,128)(2,1)}, bf16[4096,128]{1,0:T(8,128)(2,1)}, u32[]{:S(2)}, u32[]{:S(2)}) collective-permute-start(bf16[4096,128]{1,0:T(8,128)(2,1)} %get-tuple-element.18), channel_id=1, source_target_pairs={{0,2},{2,0},{4,6},{6,4},{8,10},{10,8},{12,14},{14,12},{1,3},{3,1},... | collective-permute-start | bytes 3145736 | tf_op jit(solution)/shard_map/ppermute | solution.py:553
  25.0 83.6 %collective-permute-start.4 = (bf16[4096,128]{1,0:T(8,128)(2,1)}, bf16[4096,128]{1,0:T(8,128)(2,1)}, u32[]{:S(2)}, u32[]{:S(2)}) collective-permute-start(bf16[4096,128]{1,0:T(8,128)(2,1)} %get-tuple-element.19), channel_id=1, source_target_pairs={{0,4},{2,6},{4,0},{6,2},{8,12},{10,14},{12,8},{14,10},{1,5},{3,7},... | collective-permute-start | bytes 3145736 | tf_op jit(solution)/shard_map/ppermute | solution.py:553
  26.4 105.2 %collective-permute-start.5 = (bf16[4096,128]{1,0:T(8,128)(2,1)}, bf16[4096,128]{1,0:T(8,128)(2,1)}, u32[]{:S(2)}, u32[]{:S(2)}) collective-permute-start(bf16[4096,128]{1,0:T(8,128)(2,1)} %get-tuple-element.20), channel_id=1, source_target_pairs={{0,6},{2,4},{4,2},{6,0},{8,14},{10,12},{12,10},{14,8},{1,7},{3,5},... | collective-permute-start | bytes 3145736 | tf_op jit(solution)/shard_map/ppermute | solution.py:553
  29.0 10.4 %copy-start.4 = (bf16[1,128,4,128]{3,2,1,0:T(4,128)(2,1)S(1)}, bf16[1,128,4,128]{3,2,1,0:T(4,128)(2,1)}, u32[]{:S(2)}) copy-start(bf16[1,128,4,128]{3,2,1,0:T(4,128)(2,1)} %param.16) | copy-start | bytes 393220
  29.0 11.1 %copy-start.2 = (bf16[1,128,4,128]{3,2,1,0:T(4,128)(2,1)S(1)}, bf16[1,128,4,128]{3,2,1,0:T(4,128)(2,1)}, u32[]{:S(2)}) copy-start(bf16[1,128,4,128]{3,2,1,0:T(4,128)(2,1)} %param.15) | copy-start | bytes 393220
  36.1 114.0 %collective-permute-start = (bf16[4352,128]{1,0:T(8,128)(2,1)}, bf16[4352,128]{1,0:T(8,128)(2,1)S(1)}, u32[]{:S(2)}, u32[]{:S(2)}) collective-permute-start(bf16[4352,128]{1,0:T(8,128)(2,1)} %get-tuple-element.15), channel_id=1, source_target_pairs={{0,2},{2,0},{4,6},{6,4},{8,10},{10,8},{12,14},{14,12},{1,3},{3,1},... | collective-permute-start | bytes 3342344 | tf_op jit(solution)/shard_map/ppermute | solution.py:553
  38.1 116.9 %collective-permute-start.1 = (bf16[4352,128]{1,0:T(8,128)(2,1)}, bf16[4352,128]{1,0:T(8,128)(2,1)}, u32[]{:S(2)}, u32[]{:S(2)}) collective-permute-start(bf16[4352,128]{1,0:T(8,128)(2,1)} %get-tuple-element.16), channel_id=1, source_target_pairs={{0,4},{2,6},{4,0},{6,2},{8,12},{10,14},{12,8},{14,10},{1,5},{3,7},... | collective-permute-start | bytes 3342344 | tf_op jit(solution)/shard_map/ppermute | solution.py:553
  86.1 92.2 %collective-permute-start.2 = (bf16[4352,128]{1,0:T(8,128)(2,1)}, bf16[4352,128]{1,0:T(8,128)(2,1)}, u32[]{:S(2)}, u32[]{:S(2)}) collective-permute-start(bf16[4352,128]{1,0:T(8,128)(2,1)} %get-tuple-element.17), channel_id=1, source_target_pairs={{0,6},{2,4},{4,2},{6,0},{8,14},{10,12},{12,10},{14,8},{1,7},{3,5},... | collective-permute-start | bytes 3342344 | tf_op jit(solution)/shard_map/ppermute | solution.py:553
  87.2 8.0 %copy-start.1 = (bf16[1,128,4,128]{3,2,1,0:T(4,128)(2,1)S(1)}, bf16[1,128,4,128]{3,2,1,0:T(4,128)(2,1)}, u32[]{:S(2)}) copy-start(bf16[1,128,4,128]{3,2,1,0:T(4,128)(2,1)} %param.13) | copy-start | bytes 393220
  150.1 28.3 %copy-start.6 = (bf16[4352,128]{1,0:T(8,128)(2,1)}, bf16[4352,128]{1,0:T(8,128)(2,1)S(1)}, u32[]{:S(2)}) copy-start(bf16[4352,128]{1,0:T(8,128)(2,1)S(1)} %collective-permute-done.refs_1_.refs_6_) | copy-start | bytes 3342340
  196.9 53.2 %all-to-all-start.1 = ((bf16[8,1056,128]{2,1,0:T(8,128)(2,1)}), bf16[8,1056,128]{2,1,0:T(8,128)(2,1)S(1)}, u32[]{:S(2)}, u32[]{:S(2)}) async-start(bf16[8,1056,128]{2,1,0:T(8,128)(2,1)} %get-tuple-element.22), calls=%async_computation.1 | async-start | bytes 4325376 | tf_op jit(solution)/shard_map/all_to_all | solution.py:527
  250.1 4.4 %copy-start = (bf16[8,1056,128]{2,1,0:T(8,128)(2,1)}, bf16[8,1056,128]{2,1,0:T(8,128)(2,1)S(1)}, u32[]{:S(2)}) copy-start(bf16[8,1056,128]{2,1,0:T(8,128)(2,1)S(1)} %all-to-all-done.1.part_ref.part_stat_ref) | copy-start | bytes 6488068
  250.1 53.6 %all-to-all-start.2 = ((bf16[8,1056,128]{2,1,0:T(8,128)(2,1)}), bf16[8,1056,128]{2,1,0:T(8,128)(2,1)}, u32[]{:S(2)}, u32[]{:S(2)}) async-start(bf16[8,1056,128]{2,1,0:T(8,128)(2,1)} %attend_second.1), calls=%async_computation.2 | async-start | bytes 4325376 | tf_op jit(solution)/shard_map/all_to_all | solution.py:527

commit v3 on v2

v3 whole, which is shorter than its diff:
```python
import functools

import jax
import jax.numpy as jnp
from jax import lax
from jax.experimental import pallas as pl
from jax.experimental.pallas import tpu as pltpu
from jax.sharding import PartitionSpec as P

rope_theta = 500000.0
log2_e = 1.4426950408889634
stat_rows = 32
row_tile = 256
vmem_bytes = 56 * 1024 * 1024


def rotary_tables(positions, head_width):
    half_width = head_width // 2
    frequency = rope_theta ** (-(jnp.arange(half_width, dtype=jnp.float32) * 2.0) / head_width)
    angles = positions.astype(jnp.float32)[..., None] * frequency
    cosine = jnp.cos(angles)
    sine_part = jnp.sin(angles)
    return jnp.concatenate([cosine, cosine], -1), jnp.concatenate([-sine_part, sine_part], -1)


def rotary(vector, cosine, signed_sine):
    widened = vector.astype(jnp.float32)
    swapped = jnp.roll(widened, widened.shape[-1] // 2, axis=-1)
    turned = widened * cosine[:, None, :] + swapped * signed_sine[:, None, :]
    return turned.astype(jnp.bfloat16)


def turn_kernel(head_count, copies, first_ref, second_ref, cosine_ref, sine_ref, out_ref):
    token_tile, query_heads, width = first_ref.shape[1:]
    group_size = query_heads // head_count
    rows = token_tile * group_size
    for depth, query_ref in enumerate((first_ref, second_ref)):
        widened = query_ref[0].astype(jnp.float32)
        swapped = pltpu.roll(widened.reshape(token_tile * query_heads, width), width // 2, 1)
        swapped = swapped.reshape(token_tile, query_heads, width)
        turned = widened * cosine_ref[depth][:, None, :] + swapped * sine_ref[depth][:, None, :]
        for head in range(head_count):
            turned_head = turned[:, head * group_size : (head + 1) * group_size, :]
            turned_head = turned_head.reshape(rows, width).astype(jnp.bfloat16)
            for copy in range(copies):
                out_ref[copy * head_count + head, depth] = turned_head


def turn_queries(queries_one, queries_two, cosine, sine_part, head_count, copies):
    _, token_count, query_heads, width = queries_one.shape
    token_tile = 32
    rows = token_tile * query_heads // head_count
    query_spec = pl.BlockSpec((1, token_tile, query_heads, width), lambda step: (0, step, 0, 0))
    table_spec = pl.BlockSpec((2, token_tile, width), lambda step: (0, step, 0))
    return pl.pallas_call(
        functools.partial(turn_kernel, head_count, copies),
        grid=(token_count // token_tile,),
        in_specs=[query_spec, query_spec, table_spec, table_spec],
        out_specs=pl.BlockSpec(
            (head_count * copies, 2, rows, width), lambda step: (0, 0, step, 0)
        ),
        out_shape=jax.ShapeDtypeStruct(
            (head_count * copies, 2, token_count * query_heads // head_count, width), jnp.bfloat16
        ),
        compiler_params=pltpu.CompilerParams(vmem_limit_bytes=vmem_bytes),
        cost_estimate=pl.CostEstimate(
            flops=8 * queries_one.size, bytes_accessed=12 * queries_one.size, transcendentals=0
        ),
        name="turn_queries",
    )(queries_one, queries_two, cosine, sine_part)


def local_blocks(paths, here_index, per_owner, per_peer):
    is_local = paths // per_owner == here_index
    slot_rank = jnp.cumsum(is_local.astype(jnp.int32), axis=1) - 1
    slot_range = jnp.arange(per_peer, dtype=jnp.int32)
    selected = jnp.logical_and(
        is_local[:, :, None], slot_rank[:, :, None] == slot_range[None, None, :]
    )
    return jnp.sum(jnp.where(selected, (paths % per_owner)[:, :, None], 0), axis=1)


def pack_kernel(per_peer, head_count, token_count, with_new, index_ref, place_ref, *refs):
    key_refs = refs[:per_peer]
    value_refs = refs[per_peer : 2 * per_peer]
    refs = refs[2 * per_peer :]
    new_refs = ()
    if with_new:
        new_refs = refs[:2]
    out_refs, wide = refs[-1 - head_count : -1], refs[-1]
    step = pl.program_id(0)
    mine = place_ref[0]
    span_rows = 2 * per_peer * token_count

    def spread(rows, offset):
        wide[...] = rows.astype(jnp.float32)
        for far in range(head_count):
            head = lax.bitwise_xor(mine, far)
            picked = wide[pl.ds(head, token_count, stride=head_count), :]
            out_refs[far][pl.ds(offset, token_count), :] = picked.astype(jnp.bfloat16)

    for which, source_refs in enumerate((key_refs, value_refs)):
        for slot, source in enumerate(source_refs):
            offset = step * span_rows + (which * per_peer + slot) * token_count
            spread(source[0], pl.multiple_of(offset, token_count))
    if with_new:

        @pl.when(step == 0)
        def _():
            base = pl.num_programs(0) * span_rows
            for which, source in enumerate(new_refs):
                spread(source[...], pl.multiple_of(base + which * token_count, token_count))


def pack(cache_keys, cache_values, block_index, place, new_rows, per_peer, before=()):
    block_count, token_count, head_count, width = cache_keys.shape
    flat_keys = cache_keys.reshape(block_count, token_count * head_count, width)
    flat_values = cache_values.reshape(block_count, token_count * head_count, width)
    span_rows = 2 * per_peer * token_count
    out_rows = head_count * span_rows + (2 * token_count if new_rows else 0)

    def block_spec(slot):
        return pl.BlockSpec(
            (1, token_count * head_count, width),
            lambda step, index, place: (
                index[(place[1] * head_count + step) * per_peer + slot],
                0,
                0,
            ),
        )

    cache_specs = [block_spec(slot) for slot in range(per_peer)]
    new_spec = pl.BlockSpec((token_count * head_count, width), lambda step, index, place: (0, 0))
    operands = [flat_keys] * per_peer + [flat_values] * per_peer
    operands += [row.reshape(token_count * head_count, width) for row in new_rows]
    return pl.pallas_call(
        functools.partial(pack_kernel, per_peer, head_count, token_count, bool(new_rows)),
        grid_spec=pltpu.PrefetchScalarGridSpec(
            num_scalar_prefetch=2,
            grid=(head_count,),
            in_specs=cache_specs
            + cache_specs
            + [new_spec] * len(new_rows)
            + [pl.BlockSpec(memory_space=pl.ANY)] * len(before),
            out_specs=[pl.BlockSpec((out_rows, width), lambda step, index, place: (0, 0))]
            * head_count,
            scratch_shapes=[pltpu.VMEM((token_count * head_count, width), jnp.float32)],
        ),
        out_shape=[jax.ShapeDtypeStruct((out_rows, width), jnp.bfloat16)] * head_count,
        compiler_params=pltpu.CompilerParams(vmem_limit_bytes=vmem_bytes),
        cost_estimate=pl.CostEstimate(
            flops=0, bytes_accessed=4 * head_count * out_rows * width, transcendentals=0
        ),
        name="pack_rows",
    )(block_index, place, *operands, *before)


def eye(size):
    return lax.broadcasted_iota(jnp.int32, (size, size), 0) == lax.broadcasted_iota(
        jnp.int32, (size, size), 1
    )


def product(left, right):
    return lax.dot_general(
        left, right, (((1,), (1,)), ((), ())), preferred_element_type=jnp.float32
    )


def fold_lanes(array, width, operation):
    pieces = [array[:, start : start + width] for start in range(0, array.shape[1], width)]
    while len(pieces) > 1:
        pieces = [
            operation(*pieces[start : start + 2]) if start + 1 < len(pieces) else pieces[start]
            for start in range(0, len(pieces), 2)
        ]
    return pieces[0]


def attend_task(query_of, put, row_count, width, parts, mask_of, level_ref, score_ref, score_scale):
    tile_count = row_count // row_tile

    def make_scores(tile):
        query = query_of(tile)
        top, start = None, 0
        for place, (keys, _) in enumerate(parts):
            scores = product(query, keys())
            if mask_of is not None and place == len(parts) - 1:
                scores = jnp.where(mask_of(tile), scores, -1e30)
            size = scores.shape[1]
            score_ref[tile % 2, :, start : start + size] = scores
            start += size
            folded = fold_lanes(scores, width, jnp.maximum)
            top = folded if top is None else jnp.maximum(top, folded)
        return jnp.max(top, axis=-1, keepdims=True)

    picks = eye(width)
    row_max = make_scores(0)
    for tile in range(tile_count):
        next_max = make_scores(tile + 1) if tile + 1 < tile_count else None
        total, mixture, start = None, None, 0
        for _, values in parts:
            value_rows = values()
            size = value_rows.shape[0]
            scores = score_ref[tile % 2, :, start : start + size]
            start += size
            weights = jnp.exp2((scores - row_max) * (score_scale * log2_e))
            folded = fold_lanes(weights, width, jnp.add)
            total = folded if total is None else total + folded
            mixed = jnp.dot(
                weights.astype(jnp.bfloat16), value_rows, preferred_element_type=jnp.float32
            )
            mixture = mixed if mixture is None else mixture + mixed
        total = jnp.sum(total, axis=-1, keepdims=True)
        put(tile * row_tile, (mixture / total).astype(jnp.bfloat16))
        level = row_max * score_scale + jnp.log(total)
        for piece in range(row_tile // width):
            line = jnp.where(picks, level[piece * width : (piece + 1) * width], 0.0)
            row = tile * (row_tile // width) + piece
            level_ref[row : row + 1, :] = jnp.sum(line, axis=0, keepdims=True)
        row_max = next_max
    levels = level_ref[...]
    high = levels.astype(jnp.bfloat16).astype(jnp.float32)
    middle = (levels - high).astype(jnp.bfloat16).astype(jnp.float32)
    low = levels - high - middle
    stats = jnp.concatenate([high, middle, low, jnp.zeros_like(levels)], 0)
    put(row_count, stats.astype(jnp.bfloat16))


def putter(out_ref):
    def put(start, rows):
        out_ref[start : start + rows.shape[0], :] = rows

    return put


def hand_out(stage_ref, out_refs):
    for far, out_ref in enumerate(out_refs):

        @pl.when(pl.program_id(0) == far)
        def _():
            out_ref[...] = stage_ref[...]


def tile_reader(query_ref):
    return lambda tile: query_ref[0, tile * row_tile : (tile + 1) * row_tile, :]


def task_scratch(row_count, width, key_count):
    return [
        pltpu.VMEM((row_count // width, width), jnp.float32),
        pltpu.VMEM((2, row_tile, key_count), jnp.float32),
    ]


def task_cost(task_count, row_count, key_count, width):
    return pl.CostEstimate(
        flops=4 * task_count * row_count * key_count * width,
        bytes_accessed=4 * task_count * (row_count + key_count) * width,
        transcendentals=task_count * row_count * key_count,
    )


def first_kernel(
    source_count, task_count, part_rows, score_scale, stacked, place_ref, query_ref, *refs
):
    source_refs = refs[:source_count]
    out_refs = refs[-4 - (1 if stacked else task_count) : -4]
    mark_ref, level_ref, score_ref, stage_ref = refs[-4:]
    _, row_count, width = query_ref.shape
    mark_ref[...] = jnp.zeros_like(mark_ref)
    parts = [
        (
            functools.partial(lambda ref: ref[0:part_rows, :], ref),
            functools.partial(lambda ref: ref[part_rows : 2 * part_rows, :], ref),
        )
        for ref in source_refs
    ]

    attend_task(
        tile_reader(query_ref),
        putter(out_refs[0].at[0] if stacked else stage_ref),
        row_count,
        width,
        parts,
        None,
        level_ref,
        score_ref,
        score_scale,
    )
    if not stacked:
        hand_out(stage_ref, out_refs)


def result_arrays(task_count, out_rows, width, stacked):
    if stacked:
        specs = [
            pl.BlockSpec(
                (1, out_rows, width),
                lambda step, *prefetched: (lax.bitwise_xor(prefetched[-1][0], step), 0, 0),
            )
        ]
        shapes = [jax.ShapeDtypeStruct((task_count, out_rows, width), jnp.bfloat16)]
    else:
        specs = [pl.BlockSpec((out_rows, width), lambda step, *prefetched: (0, 0))] * task_count
        shapes = [jax.ShapeDtypeStruct((out_rows, width), jnp.bfloat16)] * task_count
    specs.append(pl.BlockSpec((8, width), lambda step, *prefetched: (0, 0)))
    shapes.append(jax.ShapeDtypeStruct((8, width), jnp.float32))
    return specs, shapes


def attend_first(
    queries, sources, place, first_far, task_count, part_rows, score_scale, stacked, before
):
    _, _, row_count, width = queries.shape
    source_count = len(sources)
    out_rows = row_count + stat_rows
    out_specs, out_shape = result_arrays(task_count, out_rows, width, stacked)
    outs = pl.pallas_call(
        functools.partial(
            first_kernel, source_count, task_count, part_rows, score_scale, stacked
        ),
        grid_spec=pltpu.PrefetchScalarGridSpec(
            num_scalar_prefetch=1,
            grid=(task_count,),
            in_specs=[
                pl.BlockSpec(
                    (1, None, row_count, width),
                    lambda step, place: (
                        place[1] * source_count + lax.bitwise_xor(place[0], first_far + step),
                        0,
                        0,
                        0,
                    ),
                )
            ]
            + [
                pl.BlockSpec(
                    (2 * part_rows, width),
                    lambda step, place: (lax.bitwise_xor(place[0], first_far + step), 0),
                )
            ]
            * source_count
            + [pl.BlockSpec(memory_space=pl.ANY)] * len(before),
            out_specs=out_specs,
            scratch_shapes=task_scratch(row_count, width, source_count * part_rows)
            + [pltpu.VMEM((out_rows, width), jnp.bfloat16)],
        ),
        out_shape=out_shape,
        compiler_params=pltpu.CompilerParams(vmem_limit_bytes=vmem_bytes),
        cost_estimate=task_cost(task_count, row_count, source_count * part_rows, width),
        name="attend_first",
    )(place, queries, *sources, *before)
    return outs[:-1], outs[-1]


def second_kernel(
    chunk_count,
    source_count,
    first_far,
    task_count,
    part_rows,
    score_scale,
    stacked,
    parent_ref,
    place_ref,
    *refs,
):
    query_ref = refs[0]
    source_refs = refs[1 : 1 + chunk_count * source_count]
    out_refs = refs[-8 - (1 if stacked else task_count) : -8]
    mark_ref, level_ref, score_ref, stage_ref, held, fresh = refs[-8:-2]
    semaphores, fresh_semaphores = refs[-2:]
    _, row_count, width = query_ref.shape
    span_rows = 2 * part_rows
    token_count = fresh.shape[1] // 2
    step = pl.program_id(0)
    mine, group, home = place_ref[0], place_ref[1], place_ref[2]
    mark_ref[...] = jnp.zeros_like(mark_ref)

    def parent_at(task):
        return parent_ref[group * source_count + lax.bitwise_xor(mine, first_far + task)]

    def fetch(task):
        parent = parent_at(task)
        path = parent % source_count
        chunk_of = lax.bitwise_xor(parent // source_count, home)
        for chunk in range(chunk_count):

            @pl.when(chunk_of == chunk)
            def _():
                for source in range(source_count):
                    pltpu.make_async_copy(
                        source_refs[chunk * source_count + source].at[
                            pl.ds(pl.multiple_of(path * span_rows, span_rows), span_rows)
                        ],
                        held.at[task % 2, source],
                        semaphores.at[task % 2, source],
                    ).start()

    fresh_copies = [
        pltpu.make_async_copy(
            source_refs[source].at[pl.ds(source_count * span_rows, 2 * token_count)],
            fresh.at[source],
            fresh_semaphores.at[source],
        )
        for source in range(source_count)
    ]

    @pl.when(step == 0)
    def _():
        fetch(0)
        for copy in fresh_copies:
            copy.start()
        for copy in fresh_copies:
            copy.wait()

    @pl.when(step + 1 < task_count)
    def _():
        fetch(step + 1)

    slot = step % 2
    for source in range(source_count):
        pltpu.make_async_copy(
            source_refs[source].at[pl.ds(0, span_rows)],
            held.at[slot, source],
            semaphores.at[slot, source],
        ).wait()

    parent = parent_at(step)
    present = parent // source_count == home
    fresh_place = lax.bitwise_xor(parent % source_count, mine)
    parts = [
        (
            functools.partial(lambda source: held[slot, source, 0:part_rows, :], source),
            functools.partial(lambda source: held[slot, source, part_rows:span_rows, :], source),
        )
        for source in range(source_count)
    ]
    parts.append(
        (
            lambda: fresh[fresh_place, 0:token_count, :],
            lambda: fresh[fresh_place, token_count : 2 * token_count, :],
        )
    )

    def mask_of(tile):
        return jnp.broadcast_to(present, (row_tile, token_count))

    attend_task(
        tile_reader(query_ref),
        putter(out_refs[0].at[0] if stacked else stage_ref),
        row_count,
        width,
        parts,
        mask_of,
        level_ref,
        score_ref,
        score_scale,
    )
    if not stacked:
        hand_out(stage_ref, out_refs)


def attend_second(
    queries, chunks, parents, place, first_far, task_count, part_rows, score_scale, stacked, before
):
    _, _, row_count, width = queries.shape
    source_count = len(chunks[0])
    chunk_count = len(chunks)
    span_rows = 2 * part_rows
    fresh_rows = chunks[0][0].shape[0] - source_count * span_rows
    operands = [ref for chunk in chunks for ref in chunk]
    keys = source_count * part_rows + fresh_rows // 2
    out_rows = row_count + stat_rows
    out_specs, out_shape = result_arrays(task_count, out_rows, width, stacked)
    outs = pl.pallas_call(
        functools.partial(
            second_kernel,
            chunk_count,
            source_count,
            first_far,
            task_count,
            part_rows,
            score_scale,
            stacked,
        ),
        grid_spec=pltpu.PrefetchScalarGridSpec(
            num_scalar_prefetch=2,
            grid=(task_count,),
            in_specs=[
                pl.BlockSpec(
                    (1, None, row_count, width),
                    lambda step, parent, place: (
                        place[1] * source_count + lax.bitwise_xor(place[0], first_far + step),
                        1,
                        0,
                        0,
                    ),
                )
            ]
            + [pl.BlockSpec(memory_space=pl.ANY)] * (len(operands) + len(before)),
            out_specs=out_specs,
            scratch_shapes=task_scratch(row_count, width, keys)
            + [
                pltpu.VMEM((out_rows, width), jnp.bfloat16),
                pltpu.VMEM((2, source_count, span_rows, width), jnp.bfloat16),
                pltpu.VMEM((source_count, fresh_rows, width), jnp.bfloat16),
                pltpu.SemaphoreType.DMA((2, source_count)),
                pltpu.SemaphoreType.DMA((source_count,)),
            ],
        ),
        out_shape=out_shape,
        compiler_params=pltpu.CompilerParams(vmem_limit_bytes=vmem_bytes),
        cost_estimate=task_cost(task_count, row_count, keys, width),
        name="attend_second",
    )(parents, place, queries, *operands, *before)
    return outs[:-1], outs[-1]


def own_kernel(
    group_size, score_scale, place_ref, query_ref, key_ref, value_ref, out_ref, level_ref, score_ref
):
    token_count = key_ref.shape[1]
    _, row_count, width = query_ref.shape

    def mask_of(tile):
        row = tile * row_tile + lax.broadcasted_iota(jnp.int32, (row_tile, token_count), 0)
        column = lax.broadcasted_iota(jnp.int32, (row_tile, token_count), 1)
        return column * group_size <= row

    attend_task(
        tile_reader(query_ref),
        putter(out_ref.at[0]),
        row_count,
        width,
        [(lambda: key_ref[0], lambda: value_ref[0])],
        mask_of,
        level_ref,
        score_ref,
        score_scale,
    )


def attend_own(queries, depth, keys, values, place, score_scale):
    head_count, token_count, width = keys.shape
    row_count = queries.shape[2]

    def head_spec(rows):
        return pl.BlockSpec(
            (1, rows, width), lambda step, place: (lax.bitwise_xor(place[0], step), 0, 0)
        )

    return pl.pallas_call(
        functools.partial(own_kernel, row_count // token_count, score_scale),
        grid_spec=pltpu.PrefetchScalarGridSpec(
            num_scalar_prefetch=1,
            grid=(head_count,),
            in_specs=[
                pl.BlockSpec(
                    (1, None, row_count, width),
                    lambda step, place: (lax.bitwise_xor(place[0], step), depth, 0, 0),
                ),
                head_spec(token_count),
                head_spec(token_count),
            ],
            out_specs=pl.BlockSpec(
                (1, row_count + stat_rows, width), lambda step, place: (step, 0, 0)
            ),
            scratch_shapes=task_scratch(row_count, width, token_count),
        ),
        out_shape=jax.ShapeDtypeStruct((head_count, row_count + stat_rows, width), jnp.bfloat16),
        compiler_params=pltpu.CompilerParams(vmem_limit_bytes=vmem_bytes),
        cost_estimate=task_cost(head_count, row_count, token_count, width),
        name="attend_own",
    )(place, queries, keys, values)


def merge_kernel(head_count, group_size, part_count, place_ref, *refs):
    part_refs, own_ref = refs[:part_count], refs[part_count]
    refs = refs[part_count + 1 :]
    stat_refs, own_stat_ref = refs[:part_count], refs[part_count]
    out_ref, mixed_ref = refs[-2:]
    token_tile, _, lanes = out_ref.shape[1:]
    stat_tile = token_tile * group_size // lanes
    step = pl.program_id(0)
    picks = eye(lanes)
    ones = jnp.ones((2 * lanes, lanes), jnp.bfloat16)
    span = stat_rows // 4

    for far in range(head_count):
        head = lax.bitwise_xor(place_ref[0], far)
        sources = [part_refs[place] for place in range(far, part_count, head_count)]
        sources.append(own_ref.at[far])
        stats = [stat_refs[place][...] for place in range(far, part_count, head_count)]
        stats.append(own_stat_ref[far])
        stats = [stat.astype(jnp.float32) for stat in stats]
        level = [
            stat[:span] + stat[span : 2 * span] + stat[2 * span : 3 * span] for stat in stats
        ]
        top = functools.reduce(jnp.maximum, level)
        shares = [jnp.exp(one - top) for one in level]
        total = functools.reduce(jnp.add, shares)
        shares = [one / total for one in shares]
        lines = []
        for share in shares:
            for piece in range(stat_tile):
                chosen = (
                    lax.broadcasted_iota(jnp.int32, share.shape, 0) == step * stat_tile + piece
                )
                lines.append(jnp.sum(jnp.where(chosen, share, 0.0), axis=0, keepdims=True))
        scales = []
        for line in lines:
            high = line.astype(jnp.bfloat16).astype(jnp.float32)
            scales.append(
                jnp.concatenate(
                    [
                        jnp.where(picks, portion, 0.0).astype(jnp.bfloat16)
                        for portion in (high, line - high)
                    ],
                    1,
                )
            )
        columns = jnp.dot(
            jnp.concatenate(scales, 0), ones, preferred_element_type=jnp.float32
        )
        mixed = None
        rows = stat_tile * lanes
        for place, source in enumerate(sources):
            block = source[...].astype(jnp.float32) * columns[place * rows : (place + 1) * rows]
            mixed = block if mixed is None else mixed + block
        mixed_ref[
            :, pl.ds(pl.multiple_of(head * group_size, group_size), group_size), :
        ] = mixed.reshape(token_tile, group_size, lanes)
    out_ref[0] = mixed_ref[...].astype(out_ref.dtype)


def merge(parts, own, place, token_count, before=()):
    head_count, out_rows, width = own.shape
    row_count = out_rows - stat_rows
    group_size = row_count // token_count
    token_tile = 64
    rows = token_tile * group_size
    stat_block = row_count // stat_rows
    query_heads = head_count * group_size

    def specs(size, index):
        flat = pl.BlockSpec((size, width), lambda step, place: (index(step), 0))
        whole = pl.BlockSpec((head_count, size, width), lambda step, place: (0, index(step), 0))
        return [flat] * len(parts) + [whole]

    return pl.pallas_call(
        functools.partial(merge_kernel, head_count, group_size, len(parts)),
        grid_spec=pltpu.PrefetchScalarGridSpec(
            num_scalar_prefetch=1,
            grid=(token_count // token_tile,),
            in_specs=specs(rows, lambda step: step)
            + specs(stat_rows, lambda step: stat_block)
            + [pl.BlockSpec(memory_space=pl.ANY)] * len(before),
            out_specs=pl.BlockSpec(
                (1, token_tile, query_heads, width), lambda step, place: (0, step, 0, 0)
            ),
            scratch_shapes=[pltpu.VMEM((token_tile, query_heads, width), jnp.float32)],
        ),
        out_shape=jax.ShapeDtypeStruct((1, token_count, query_heads, width), jnp.bfloat16),
        compiler_params=pltpu.CompilerParams(vmem_limit_bytes=vmem_bytes),
        cost_estimate=pl.CostEstimate(
            flops=4 * (len(parts) + head_count) * row_count * width,
            bytes_accessed=4 * (len(parts) + head_count) * row_count * width,
            transcendentals=0,
        ),
        name="merge_parts",
    )(place, *parts, own, *parts, own, *before)


def local(
    queries_one,
    keys_one,
    values_one,
    queries_two,
    keys_two,
    values_two,
    cache_keys,
    cache_values,
    paths,
    parents,
    positions,
):
    here_index = lax.axis_index("node")
    peer_count = lax.axis_size("node")
    block_count, token_count, head_count, width = cache_keys.shape
    per_peer = paths.shape[1] // peer_count
    copies = peer_count // head_count
    score_scale = width ** (-0.5)
    my_head = here_index % head_count
    my_group = here_index // head_count
    part_rows = per_peer * token_count
    places = [
        jnp.stack([my_head, lax.bitwise_xor(my_group, apart), my_group]) for apart in range(copies)
    ]

    def swap(array, apart):
        return lax.ppermute(array, "node", [(node, node ^ apart) for node in range(peer_count)])

    cosine, sine_part = rotary_tables(positions[:, 0], width)
    send = turn_queries(queries_one, queries_two, cosine, sine_part, head_count, copies)
    got = lax.all_to_all(send, "node", split_axis=0, concat_axis=0, tiled=True)
    key_rot_one = rotary(keys_one[0], cosine[0], sine_part[0])
    key_rot_two = rotary(keys_two[0], cosine[1], sine_part[1])

    block_index = local_blocks(paths, here_index, block_count, per_peer).reshape(-1)
    order = list(range(1, copies)) + [0]
    chunks = [None] * copies
    before = (send,)
    for apart in order:
        packed = pack(
            cache_keys,
            cache_values,
            block_index,
            places[apart],
            () if apart else (key_rot_one, values_one[0]),
            per_peer,
            before,
        )
        chunks[apart] = [packed[0]] + [swap(packed[far], far) for far in range(1, head_count)]
        before = (packed[0],)

    own_one = attend_own(
        send,
        0,
        jnp.moveaxis(key_rot_one, 1, 0),
        jnp.moveaxis(values_one[0], 1, 0),
        places[0],
        score_scale,
    )
    own_two = attend_own(
        send,
        1,
        jnp.moveaxis(key_rot_two, 1, 0),
        jnp.moveaxis(values_two[0], 1, 0),
        places[0],
        score_scale,
    )

    def send_home(apart, first_far, rows):
        base = apart * head_count + first_far
        return [swap(row, base + far) for far, row in enumerate(rows)]

    def first(apart, first_far, task_count, stacked, before):
        rows, mark = attend_first(
            got,
            chunks[apart],
            places[apart],
            first_far,
            task_count,
            part_rows,
            score_scale,
            stacked,
            before,
        )
        return rows, (mark,)

    def second(apart, first_far, task_count, stacked, before):
        rows, mark = attend_second(
            got,
            chunks,
            parents,
            places[apart],
            first_far,
            task_count,
            part_rows,
            score_scale,
            stacked,
            before,
        )
        return rows, (mark,)

    far_one, far_two = [], []
    before = (own_one, own_two)
    for apart in order[:-1]:
        rows, before = first(apart, 0, 1, False, before)
        far_one += send_home(apart, 0, rows)
        rows, before = first(apart, 1, head_count - 1, False, before)
        far_one += send_home(apart, 1, rows)
    for number, apart in enumerate(order[:-1]):
        rows, before = second(apart, 0, 1, False, before)
        far_two += send_home(apart, 0, rows)
        arrived = far_one[number * head_count : (number + 1) * head_count]
        rows, before = second(apart, 1, head_count - 1, False, (*before, *arrived[:2]))
        far_two += send_home(apart, 1, rows)
        before = (*before, *arrived[2:])
    rows, before = first(0, 1, head_count - 1, False, before)
    near_one = send_home(0, 1, rows)
    rows, before = second(0, 1, head_count - 1, False, (*before, *far_two[:2]))
    near_two = send_home(0, 1, rows)
    rows, before = first(0, 0, 1, False, before)
    near_one = [*rows, *near_one]
    rows, before = second(0, 0, 1, False, before)
    near_two = [*rows, *near_two]
    before = (*before, far_two[2])
    return (
        merge(far_one + near_one, own_one, places[0], token_count, before),
        merge(far_two + near_two, own_two, places[0], token_count),
    )


def solution(mesh):
    in_specs = (
        P(("group", "node"), None, "head", None),
        P(("group", "node"), None, "head", None),
        P(("group", "node"), None, "head", None),
        P(("group", "node"), None, "head", None),
        P(("group", "node"), None, "head", None),
        P(("group", "node"), None, "head", None),
        P(("group", "node"), None, "head", None),
        P(("group", "node"), None, "head", None),
        P("group", None),
        P("group"),
        P(None, ("group", "node"), None),
    )
    out_specs = (P(("group", "node"), None, "head", None), P(("group", "node"), None, "head", None))
    return jax.shard_map(
        local,
        mesh=mesh,
        in_specs=in_specs,
        out_specs=out_specs,
        check_vma=False,
    )
```

time: 309 us -> 289 us (0.935)
  waiting for transfers between devices: 151 us -> 119 us
  starting transfers between devices: 23.5 us -> 35.4 us
  Pallas kernels: 124 us -> 119 us
  local copies, waits for them, and re-layouts: 3.75 us -> 7.9 us
    all_to_all x3 -> x1, waiting for transfers between devices: 50.7 us -> 0.01 us  [local(): got = lax.all_to_all(send, 'node', split_axis=0, concat_axis=0, tiled=True)]
    ppermute x6 -> x20, starting transfers between devices: 7.97 us -> 28 us  [swap(): lax.ppermute(array, 'node', [(node, node ^ apart) for node in range(peer_...]
    ppermute x6 -> x20, waiting for transfers between devices: 100 us -> 119 us  [swap(): lax.ppermute(array, 'node', [(node, node ^ apart) for node in range(peer_...]
    all_to_all x3 -> x1, starting transfers between devices: 15.6 us -> 7.41 us  [local(): got = lax.all_to_all(send, 'node', split_axis=0, concat_axis=0, tiled=True)]
    pallas_call x2, Pallas kernels: 15.9 us -> 10.4 us  [attend_own(): pl.pallas_call(functools.partial(own_kernel, row_count // token_count, sc...]
    unnamed x16 -> x48, local copies, waits for them, and re-layouts: 1.37 us -> 6.3 us
    pallas_call x1 -> x4, Pallas kernels: 42.6 us -> 43.2 us  [attend_second(): pl.pallas_call(functools.partial(second_kernel, chunk_count, source_count...]
    pallas_call x4 -> x6, Pallas kernels: 46.4 us -> 46.2 us  [the longest x4 35.8 us: attend_first(): pl.pallas_call(functools.partial(first_kernel, source_count, task_count,...]
  transfers between devices with their start and end apart: 9 -> 21, of which waited for: 7 -> 7; matrix products, arithmetic and copies ran while one was open for 2% -> 2% of each run, Pallas kernels for 31% -> 38%
where the time goes in v3:
time: 289 us; the launch traced here: 288 us
  Pallas kernels  119 us (41%)
  waiting for transfers between devices  119 us (41%)
  starting transfers between devices  35.4 us (12%)
  local copies, waits for them, and re-layouts  7.9 us (3%)
  other arithmetic  6.25 us (2%)
    ppermute x20, waiting for transfers between devices, swap(): lax.ppermute(array, 'node', [(node, node ^ apart) for node in range(peer_...  119 us
    pallas_call x4, Pallas kernels, attend_second(): pl.pallas_call(functools.partial(second_kernel, chunk_count, source_count...  43.2 us
    pallas_call x4, Pallas kernels, attend_first(): pl.pallas_call(functools.partial(first_kernel, source_count, task_count,...  35.8 us
    ppermute x20, starting transfers between devices, swap(): lax.ppermute(array, 'node', [(node, node ^ apart) for node in range(peer_...  28 us
    pallas_call x2, Pallas kernels, pack(): pl.pallas_call(functools.partial(pack_kernel, per_peer, head_count, token...  14.2 us
    pallas_call x2, Pallas kernels, merge(): pl.pallas_call(functools.partial(merge_kernel, head_count, group_size, le...  10.4 us
    pallas_call x2, Pallas kernels, attend_own(): pl.pallas_call(functools.partial(own_kernel, row_count // token_count, sc...  10.4 us
    all_to_all x1, starting transfers between devices, local(): got = lax.all_to_all(send, 'node', split_axis=0, concat_axis=0, tiled=True)  7.41 us
  transfers between devices with their start and end apart: 21, of which 7 were waited for; matrix products, arithmetic and copies ran while one was open for 2% of the time, Pallas kernels for 38%

profile of v3, /device:TPU:0, one launch (start us, length us, event | category | flops | bytes accessed | tf_op | source)
XLA Modules:
  0.0 288.2 jit_solution(9413285295636401858)
XLA Ops:
  0.6 0.7 convert_element_type.40
  1.9 0.8 pad_maximum_fusion
  2.7 4.7 %turn_queries.1.refs_8_.query_ref = bf16[8,2,1024,128]{3,2,1,0:T(8,128)(2,1)} custom-call(bf16[1,128,32,128]{3,2,1,0:T(8,128)(2,1)} %first_ref.1, bf16[1,128,32,128]{3,2,1,0:T(8,128)(2,1)} %second_ref.1, f32[2,128,128]{2,1,0:T(8,128)} %get-tuple-element.81.cosine_ref, f32[2,128,128]{2,1,0:T(8,128)} %get-tuple-element.82.sine_ref), custom_call_target="tpu_custom_call" | custom-call | flops 4194304 | bytes 6291456 | tf_op jit(solution)/shard_map/turn_queries/pallas_call | solution.py:55
  7.4 7.4 %all-to-all-start = ((bf16[8,2,1024,128]{3,2,1,0:T(8,128)(2,1)}), bf16[8,2,1024,128]{3,2,1,0:T(8,128)(2,1)}, u32[]{:S(2)}, u32[]{:S(2)}) async-start(bf16[8,2,1024,128]{3,2,1,0:T(8,128)(2,1)} %turn_queries.1.refs_8_.query_ref), calls=%async_computation | async-start | bytes 8388608 | tf_op jit(solution)/shard_map/all_to_all | solution.py:707
  16.5 7.0 %pack_rows.2 = (bf16[4096,128]{1,0:T(8,128)(2,1)}, bf16[4096,128]{1,0:T(8,128)(2,1)}, bf16[4096,128]{1,0:T(8,128)(2,1)}, bf16[4096,128]{1,0:T(8,128)(2,1)}) custom-call(s32[32]{0:T(128)} %reshape.53.index_ref, s32[3]{0:T(128)} %add_add_fusion.1.place_ref, bf16[32,512,128]{2,1,0:T(8,128)(2,1)} %bitcast.43, bf16[32,512,128]{2,1,0:T(8,128)(2,1)} %bitcast.44, ...), custom_call_target="tpu_custom_call" | custom-call | bytes 8388608 | tf_op jit(solution)/shard_map/pack_rows/pallas_call | solution.py:136
  23.5 1.8 collective-permute-start
  25.4 1.7 collective-permute-start.1
  28.0 0.8 fusion.5.refs_8_
  29.5 7.2 %pack_rows.3 = (bf16[4352,128]{1,0:T(8,128)(2,1)}, bf16[4352,128]{1,0:T(8,128)(2,1)}, bf16[4352,128]{1,0:T(8,128)(2,1)}, bf16[4352,128]{1,0:T(8,128)(2,1)}) custom-call(s32[32]{0:T(128)} %reshape.53.index_ref, s32[3]{0:T(128)} %add_add_fusion.place_ref, bf16[32,512,128]{2,1,0:T(8,128)(2,1)} %bitcast.47, bf16[32,512,128]{2,1,0:T(8,128)(2,1)} %bitcast.48, ...), custom_call_target="tpu_custom_call" | custom-call | bytes 8912896 | tf_op jit(solution)/shard_map/pack_rows/pallas_call | solution.py:136
  36.7 1.7 collective-permute-start.7
  38.4 1.8 collective-permute-start.8
  40.2 45.8 %collective-permute-done.refs_1_.refs_6_ = bf16[4096,128]{1,0:T(8,128)(2,1)S(1)} collective-permute-done((bf16[4096,128]{1,0:T(8,128)(2,1)}, bf16[4096,128]{1,0:T(8,128)(2,1)S(1)}, u32[]{:S(2)}, u32[]{:S(2)}) %collective-permute-start) | collective-permute-done | bytes 1048608 | tf_op jit(solution)/shard_map/ppermute | solution.py:703
  86.0 1.0 collective-permute-start.9
  87.2 0.7 copy.54
  87.9 0.7 copy.53
  88.6 0.8 fusion.6.key_ref
  89.4 5.2 %attend_own.3.refs_5_.refs_8_.refs_17_ = bf16[4,1056,128]{2,1,0:T(8,128)(2,1)} custom-call(s32[3]{0:T(128)} %add_add_fusion.place_ref, bf16[8,2,1024,128]{3,2,1,0:T(8,128)(2,1)} %turn_queries.1.refs_8_.query_ref, bf16[4,128,128]{2,1,0:T(8,128)(2,1)} %fusion.6.key_ref, bf16[4,128,128]{2,1,0:T(8,128)(2,1)} %bitcast.66), custom_call_target="tpu_custom_call" | custom-call | flops 268435456 | bytes 2359296 | tf_op jit(solution)/shard_map/attend_own/pallas_call | solution.py:554
  94.6 0.8 fusion.7.key_ref
  95.3 5.2 %attend_own.2.refs_4_.refs_8_.refs_17_ = bf16[4,1056,128]{2,1,0:T(8,128)(2,1)} custom-call(s32[3]{0:T(128)} %add_add_fusion.place_ref, bf16[8,2,1024,128]{3,2,1,0:T(8,128)(2,1)} %turn_queries.1.refs_8_.query_ref, bf16[4,128,128]{2,1,0:T(8,128)(2,1)} %fusion.7.key_ref, bf16[4,128,128]{2,1,0:T(8,128)(2,1)} %bitcast.65), custom_call_target="tpu_custom_call" | custom-call | flops 268435456 | bytes 2359296 | tf_op jit(solution)/shard_map/attend_own/pallas_call | solution.py:554
  100.5 8.1 %collective-permute-done.1.refs_2_.refs_7_ = bf16[4096,128]{1,0:T(8,128)(2,1)} collective-permute-done((bf16[4096,128]{1,0:T(8,128)(2,1)}, bf16[4096,128]{1,0:T(8,128)(2,1)}, u32[]{:S(2)}, u32[]{:S(2)}) %collective-permute-start.1) | collective-permute-done | bytes 1048608 | tf_op jit(solution)/shard_map/ppermute | solution.py:703
  108.6 23.0 %collective-permute-done.2.refs_3_.refs_8_ = bf16[4096,128]{1,0:T(8,128)(2,1)} collective-permute-done((bf16[4096,128]{1,0:T(8,128)(2,1)}, bf16[4096,128]{1,0:T(8,128)(2,1)}, u32[]{:S(2)}, u32[]{:S(2)}) %collective-permute-start.2) | collective-permute-done | bytes 1048608 | tf_op jit(solution)/shard_map/ppermute | solution.py:703
  131.7 5.8 %attend_first.4 = (bf16[1056,128]{1,0:T(8,128)(2,1)}, f32[8,128]{1,0:T(8,128)}) custom-call(s32[3]{0:T(128)} %add_add_fusion.1.place_ref, bf16[8,2,1024,128]{3,2,1,0:T(8,128)(2,1)} %all-to-all-done.query_ref.refs_0_, bf16[4096,128]{1,0:T(8,128)(2,1)} %get-tuple-element.34.refs_0_.refs_10_.refs_5_, bf16[4096,128]{1,0:T(8,128)(2,1)} %copy-done.3, ...), custom_call_target="tpu_custom_call" | custom-call | flops 1073741824 | bytes 1572864 | tf_op jit(solution)/shard_map/attend_first/pallas_call | solution.py:319
  137.4 2.9 collective-permute-start.3
  140.3 12.1 %attend_first.5 = (bf16[1056,128]{1,0:T(8,128)(2,1)}, bf16[1056,128]{1,0:T(8,128)(2,1)}, bf16[1056,128]{1,0:T(8,128)(2,1)}, f32[8,128]{1,0:T(8,128)}) custom-call(s32[3]{0:T(128)} %add_add_fusion.1.place_ref, bf16[8,2,1024,128]{3,2,1,0:T(8,128)(2,1)} %all-to-all-done.query_ref.refs_0_, bf16[4096,128]{1,0:T(8,128)(2,1)} %get-tuple-element.34.refs_0_.refs_10_.refs_5_, ...), custom_call_target="tpu_custom_call" | custom-call | flops 3221225472 | bytes 4718592 | tf_op jit(solution)/shard_map/attend_first/pallas_call | solution.py:319
  152.8 1.5 collective-permute-start.5
  154.3 12.1 %collective-permute-done.8.refs_3_.refs_2_ = bf16[4352,128]{1,0:T(8,128)(2,1)S(1)} collective-permute-done((bf16[4352,128]{1,0:T(8,128)(2,1)}, bf16[4352,128]{1,0:T(8,128)(2,1)S(1)}, u32[]{:S(2)}, u32[]{:S(2)}) %collective-permute-start.8) | collective-permute-done | bytes 1114144 | tf_op jit(solution)/shard_map/ppermute | solution.py:703
  166.5 3.2 %collective-permute-start.6 = (bf16[1056,128]{1,0:T(8,128)(2,1)}, bf16[1056,128]{1,0:T(8,128)(2,1)S(1)}, u32[]{:S(2)}, u32[]{:S(2)}) collective-permute-start(bf16[1056,128]{1,0:T(8,128)(2,1)} %get-tuple-element.42), channel_id=1, source_target_pairs={{0,14},{2,12},{4,10},{6,8},{8,6},{10,4},{12,2},{14,0},{1,15},{3,13... | collective-permute-start | bytes 811016 | tf_op jit(solution)/shard_map/ppermute | solution.py:703
  169.7 20.1 %collective-permute-done.9.refs_4_.refs_3_ = bf16[4352,128]{1,0:T(8,128)(2,1)S(1)} collective-permute-done((bf16[4352,128]{1,0:T(8,128)(2,1)}, bf16[4352,128]{1,0:T(8,128)(2,1)S(1)}, u32[]{:S(2)}, u32[]{:S(2)}) %collective-permute-start.9) | collective-permute-done | bytes 1114144 | tf_op jit(solution)/shard_map/ppermute | solution.py:703
  189.8 1.0 copy-done.2
  190.9 7.1 %attend_second.4 = (bf16[1056,128]{1,0:T(8,128)(2,1)}, f32[8,128]{1,0:T(8,128)}) custom-call(s32[8]{0:T(128)} %parent_ref.7, s32[3]{0:T(128)} %add_add_fusion.1.place_ref, bf16[8,2,1024,128]{3,2,1,0:T(8,128)(2,1)} %all-to-all-done.query_ref.refs_0_, bf16[4352,128]{1,0:T(8,128)(2,1)} %get-tuple-element.43.refs_1_.refs_0_, bf16[4352,128]{1,0:T(8,128)(2,1)} %copy-done, ...), custom_call_target="tpu_custom_call" | custom-call | flops 1140850688 | bytes 1638400 | tf_op jit(solution)/shard_map/attend_second/pallas_call | solution.py:477
  198.0 0.7 copy-done.4
  198.9 14.5 %attend_second.5 = (bf16[1056,128]{1,0:T(8,128)(2,1)}, bf16[1056,128]{1,0:T(8,128)(2,1)}, bf16[1056,128]{1,0:T(8,128)(2,1)}, f32[8,128]{1,0:T(8,128)}) custom-call(s32[8]{0:T(128)} %parent_ref.7, s32[3]{0:T(128)} %add_add_fusion.1.place_ref, bf16[8,2,1024,128]{3,2,1,0:T(8,128)(2,1)} %all-to-all-done.query_ref.refs_0_, ...), custom_call_target="tpu_custom_call" | custom-call | flops 3422552064 | bytes 4915200 | tf_op jit(solution)/shard_map/attend_second/pallas_call | solution.py:477
  213.4 3.0 %collective-permute-start.11 = (bf16[1056,128]{1,0:T(8,128)(2,1)}, bf16[1056,128]{1,0:T(8,128)(2,1)S(1)}, u32[]{:S(2)}, u32[]{:S(2)}) collective-permute-start(bf16[1056,128]{1,0:T(8,128)(2,1)} %get-tuple-element.52), channel_id=1, source_target_pairs={{0,10},{2,8},{4,14},{6,12},{8,2},{10,0},{12,6},{14,4},{1,11},{3,9}... | collective-permute-start | bytes 811016 | tf_op jit(solution)/shard_map/ppermute | solution.py:703
  216.3 2.0 collective-permute-start.15
  218.4 2.6 collective-permute-start.16
  221.0 0.7 copy-done.10
  221.7 12.2 %attend_first.6 = (bf16[1056,128]{1,0:T(8,128)(2,1)}, bf16[1056,128]{1,0:T(8,128)(2,1)}, bf16[1056,128]{1,0:T(8,128)(2,1)}, f32[8,128]{1,0:T(8,128)}) custom-call(s32[3]{0:T(128)} %add_add_fusion.place_ref, bf16[8,2,1024,128]{3,2,1,0:T(8,128)(2,1)} %all-to-all-done.query_ref.refs_0_, bf16[4352,128]{1,0:T(8,128)(2,1)} %get-tuple-element.43.refs_1_.refs_0_, ...), custom_call_target="tpu_custom_call" | custom-call | flops 3221225472 | bytes 4718592 | tf_op jit(solution)/shard_map/attend_first/pallas_call | solution.py:319
  234.5 2.8 collective-permute-done.10.refs_10_.refs_0_.refs_9_
  237.3 6.8 %collective-permute-done.11.refs_11_.refs_1_.refs_10_ = bf16[1056,128]{1,0:T(8,128)(2,1)S(1)} collective-permute-done((bf16[1056,128]{1,0:T(8,128)(2,1)}, bf16[1056,128]{1,0:T(8,128)(2,1)S(1)}, u32[]{:S(2)}, u32[]{:S(2)}) %collective-permute-start.11) | collective-permute-done | bytes 270368 | tf_op jit(solution)/shard_map/ppermute | solution.py:703
  244.1 0.7 copy-done.7
  244.8 14.6 %attend_second.6 = (bf16[1056,128]{1,0:T(8,128)(2,1)}, bf16[1056,128]{1,0:T(8,128)(2,1)}, bf16[1056,128]{1,0:T(8,128)(2,1)}, f32[8,128]{1,0:T(8,128)}) custom-call(s32[8]{0:T(128)} %parent_ref.7, s32[3]{0:T(128)} %add_add_fusion.place_ref, bf16[8,2,1024,128]{3,2,1,0:T(8,128)(2,1)} %all-to-all-done.query_ref.refs_0_, ...), custom_call_target="tpu_custom_call" | custom-call | flops 3422552064 | bytes 4915200 | tf_op jit(solution)/shard_map/attend_second/pallas_call | solution.py:477
  260.1 2.2 collective-permute-start.18
  262.3 0.7 collective-permute-start.19
  263.0 5.8 %attend_first.7 = (bf16[1056,128]{1,0:T(8,128)(2,1)}, f32[8,128]{1,0:T(8,128)}) custom-call(s32[3]{0:T(128)} %add_add_fusion.place_ref, bf16[8,2,1024,128]{3,2,1,0:T(8,128)(2,1)} %all-to-all-done.query_ref.refs_0_, bf16[4352,128]{1,0:T(8,128)(2,1)} %get-tuple-element.43.refs_1_.refs_0_, bf16[4352,128]{1,0:T(8,128)(2,1)} %copy-done, ...), custom_call_target="tpu_custom_call" | custom-call | flops 1073741824 | bytes 1572864 | tf_op jit(solution)/shard_map/attend_first/pallas_call | solution.py:319
  268.8 7.0 %attend_second.7 = (bf16[1056,128]{1,0:T(8,128)(2,1)}, f32[8,128]{1,0:T(8,128)}) custom-call(s32[8]{0:T(128)} %parent_ref.7, s32[3]{0:T(128)} %add_add_fusion.place_ref, bf16[8,2,1024,128]{3,2,1,0:T(8,128)(2,1)} %all-to-all-done.query_ref.refs_0_, bf16[4352,128]{1,0:T(8,128)(2,1)} %get-tuple-element.43.refs_1_.refs_0_, bf16[4352,128]{1,0:T(8,128)(2,1)} %copy-done, ...), custom_call_target="tpu_custom_call" | custom-call | flops 1140850688 | bytes 1638400 | tf_op jit(solution)/shard_map/attend_second/pallas_call | solution.py:477
  275.9 0.7 copy-done.16
  276.6 5.2 %merge_parts.2 = bf16[1,128,32,128]{3,2,1,0:T(8,128)(2,1)} custom-call(s32[3]{0:T(128)} %add_add_fusion.place_ref, bf16[1056,128]{1,0:T(8,128)(2,1)} %copy-done.4, bf16[1056,128]{1,0:T(8,128)(2,1)} %copy-done.5, bf16[1056,128]{1,0:T(8,128)(2,1)} %copy-done.9, bf16[1056,128]{1,0:T(8,128)(2,1)} %copy-done.10, ...), custom_call_target="tpu_custom_call" | custom-call | flops 6291456 | bytes 6291456 | tf_op jit(solution)/shard_map/merge_parts/pallas_call | solution.py:652
  282.8 5.2 %merge_parts.3 = bf16[1,128,32,128]{3,2,1,0:T(8,128)(2,1)} custom-call(s32[3]{0:T(128)} %add_add_fusion.place_ref, bf16[1056,128]{1,0:T(8,128)(2,1)} %copy-done.6, bf16[1056,128]{1,0:T(8,128)(2,1)} %copy-done.7, bf16[1056,128]{1,0:T(8,128)(2,1)} %copy-done.8, bf16[1056,128]{1,0:T(8,128)(2,1)} %copy-done.11, ...), custom_call_target="tpu_custom_call" | custom-call | flops 6291456 | bytes 6291456 | tf_op jit(solution)/shard_map/merge_parts/pallas_call | solution.py:652
  (82 shorter events, 6.9 us)
Async XLA Ops:
  7.4 7.4 %copy-start.22 = (s32[8,32]{1,0:T(8,128)S(1)}, s32[8,32]{1,0:T(8,128)}, u32[]{:S(2)}) copy-start(s32[8,32]{1,0:T(8,128)} %param.19) | copy-start | bytes 3076
  7.4 124.3 %all-to-all-start = ((bf16[8,2,1024,128]{3,2,1,0:T(8,128)(2,1)}), bf16[8,2,1024,128]{3,2,1,0:T(8,128)(2,1)}, u32[]{:S(2)}, u32[]{:S(2)}) async-start(bf16[8,2,1024,128]{3,2,1,0:T(8,128)(2,1)} %turn_queries.1.refs_8_.query_ref), calls=%async_computation | async-start | bytes 8388608 | tf_op jit(solution)/shard_map/all_to_all | solution.py:707
  16.5 10.5 %copy-start.20 = (bf16[1,128,4,128]{3,2,1,0:T(4,128)(2,1)S(1)}, bf16[1,128,4,128]{3,2,1,0:T(4,128)(2,1)}, u32[]{:S(2)}) copy-start(bf16[1,128,4,128]{3,2,1,0:T(4,128)(2,1)} %param.12) | copy-start | bytes 393220
  23.5 62.5 %collective-permute-start = (bf16[4096,128]{1,0:T(8,128)(2,1)}, bf16[4096,128]{1,0:T(8,128)(2,1)S(1)}, u32[]{:S(2)}, u32[]{:S(2)}) collective-permute-start(bf16[4096,128]{1,0:T(8,128)(2,1)} %get-tuple-element.35), channel_id=1, source_target_pairs={{0,2},{2,0},{4,6},{6,4},{8,10},{10,8},{12,14},{14,12},{1,3},{3,1},... | collective-permute-start | bytes 3145736 | tf_op jit(solution)/shard_map/ppermute | solution.py:703
  25.4 83.3 %collective-permute-start.1 = (bf16[4096,128]{1,0:T(8,128)(2,1)}, bf16[4096,128]{1,0:T(8,128)(2,1)}, u32[]{:S(2)}, u32[]{:S(2)}) collective-permute-start(bf16[4096,128]{1,0:T(8,128)(2,1)} %get-tuple-element.36), channel_id=1, source_target_pairs={{0,4},{2,6},{4,0},{6,2},{8,12},{10,14},{12,8},{14,10},{1,5},{3,7},... | collective-permute-start | bytes 3145736 | tf_op jit(solution)/shard_map/ppermute | solution.py:703
  27.0 104.6 %collective-permute-start.2 = (bf16[4096,128]{1,0:T(8,128)(2,1)}, bf16[4096,128]{1,0:T(8,128)(2,1)}, u32[]{:S(2)}, u32[]{:S(2)}) collective-permute-start(bf16[4096,128]{1,0:T(8,128)(2,1)} %get-tuple-element.37), channel_id=1, source_target_pairs={{0,6},{2,4},{4,2},{6,0},{8,14},{10,12},{12,10},{14,8},{1,7},{3,5},... | collective-permute-start | bytes 3145736 | tf_op jit(solution)/shard_map/ppermute | solution.py:703
  29.5 10.8 %copy-start.19 = (bf16[1,128,4,128]{3,2,1,0:T(4,128)(2,1)S(1)}, bf16[1,128,4,128]{3,2,1,0:T(4,128)(2,1)}, u32[]{:S(2)}) copy-start(bf16[1,128,4,128]{3,2,1,0:T(4,128)(2,1)} %param.15) | copy-start | bytes 393220
  36.6 50.6 %copy-start.18 = (bf16[1,128,4,128]{3,2,1,0:T(4,128)(2,1)S(1)}, bf16[1,128,4,128]{3,2,1,0:T(4,128)(2,1)}, u32[]{:S(2)}) copy-start(bf16[1,128,4,128]{3,2,1,0:T(4,128)(2,1)} %param.13) | copy-start | bytes 393220
  36.7 51.2 %copy-start.21 = (bf16[1,128,4,128]{3,2,1,0:T(4,128)(2,1)S(1)}, bf16[1,128,4,128]{3,2,1,0:T(4,128)(2,1)}, u32[]{:S(2)}) copy-start(bf16[1,128,4,128]{3,2,1,0:T(4,128)(2,1)} %param.16) | copy-start | bytes 393220
  36.7 116.2 %collective-permute-start.7 = (bf16[4352,128]{1,0:T(8,128)(2,1)}, bf16[4352,128]{1,0:T(8,128)(2,1)S(1)}, u32[]{:S(2)}, u32[]{:S(2)}) collective-permute-start(bf16[4352,128]{1,0:T(8,128)(2,1)} %get-tuple-element.44), channel_id=1, source_target_pairs={{0,2},{2,0},{4,6},{6,4},{8,10},{10,8},{12,14},{14,12},{1,3},{3,1},... | collective-permute-start | bytes 3342344 | tf_op jit(solution)/shard_map/ppermute | solution.py:703
  38.4 128.1 %collective-permute-start.8 = (bf16[4352,128]{1,0:T(8,128)(2,1)}, bf16[4352,128]{1,0:T(8,128)(2,1)S(1)}, u32[]{:S(2)}, u32[]{:S(2)}) collective-permute-start(bf16[4352,128]{1,0:T(8,128)(2,1)} %get-tuple-element.45), channel_id=1, source_target_pairs={{0,4},{2,6},{4,0},{6,2},{8,12},{10,14},{12,8},{14,10},{1,5},{3,7},... | collective-permute-start | bytes 3342344 | tf_op jit(solution)/shard_map/ppermute | solution.py:703
  86.0 3.3 %copy-start.3 = (bf16[4096,128]{1,0:T(8,128)(2,1)}, bf16[4096,128]{1,0:T(8,128)(2,1)S(1)}, u32[]{:S(2)}) copy-start(bf16[4096,128]{1,0:T(8,128)(2,1)S(1)} %collective-permute-done.refs_1_.refs_6_) | copy-start | bytes 3145732
  86.0 103.8 %collective-permute-start.9 = (bf16[4352,128]{1,0:T(8,128)(2,1)}, bf16[4352,128]{1,0:T(8,128)(2,1)S(1)}, u32[]{:S(2)}, u32[]{:S(2)}) collective-permute-start(bf16[4352,128]{1,0:T(8,128)(2,1)} %get-tuple-element.46), channel_id=1, source_target_pairs={{0,6},{2,4},{4,2},{6,0},{8,14},{10,12},{12,10},{14,8},{1,7},{3,5},... | collective-permute-start | bytes 3342344 | tf_op jit(solution)/shard_map/ppermute | solution.py:703
  137.4 60.6 %collective-permute-start.3 = (bf16[1056,128]{1,0:T(8,128)(2,1)}, bf16[1056,128]{1,0:T(8,128)(2,1)S(1)}, u32[]{:S(2)}, u32[]{:S(2)}) collective-permute-start(bf16[1056,128]{1,0:T(8,128)(2,1)} %get-tuple-element.38), channel_id=1, source_target_pairs={{0,8},{2,10},{4,12},{6,14},{8,0},{10,2},{12,4},{14,6},{1,9},{3,11}... | collective-permute-start | bytes 811016 | tf_op jit(solution)/shard_map/ppermute | solution.py:703
  152.4 45.6 %collective-permute-start.4 = (bf16[1056,128]{1,0:T(8,128)(2,1)}, bf16[1056,128]{1,0:T(8,128)(2,1)S(1)}, u32[]{:S(2)}, u32[]{:S(2)}) collective-permute-start(bf16[1056,128]{1,0:T(8,128)(2,1)} %get-tuple-element.40), channel_id=1, source_target_pairs={{0,10},{2,8},{4,14},{6,12},{8,2},{10,0},{12,6},{14,4},{1,11},{3,9}... | collective-permute-start | bytes 811016 | tf_op jit(solution)/shard_map/ppermute | solution.py:703
  152.8 37.0 %copy-start = (bf16[4352,128]{1,0:T(8,128)(2,1)}, bf16[4352,128]{1,0:T(8,128)(2,1)S(1)}, u32[]{:S(2)}) copy-start(bf16[4352,128]{1,0:T(8,128)(2,1)S(1)} %collective-permute-done.7.refs_2_.refs_1_) | copy-start | bytes 3342340
  152.8 65.5 %collective-permute-start.5 = (bf16[1056,128]{1,0:T(8,128)(2,1)}, bf16[1056,128]{1,0:T(8,128)(2,1)S(1)}, u32[]{:S(2)}, u32[]{:S(2)}) collective-permute-start(bf16[1056,128]{1,0:T(8,128)(2,1)} %get-tuple-element.41), channel_id=1, source_target_pairs={{0,12},{2,14},{4,8},{6,10},{8,4},{10,6},{12,0},{14,2},{1,13},{3,15... | collective-permute-start | bytes 811016 | tf_op jit(solution)/shard_map/ppermute | solution.py:703
  166.5 23.4 %copy-start.1 = (bf16[4352,128]{1,0:T(8,128)(2,1)}, bf16[4352,128]{1,0:T(8,128)(2,1)S(1)}, u32[]{:S(2)}) copy-start(bf16[4352,128]{1,0:T(8,128)(2,1)S(1)} %collective-permute-done.8.refs_3_.refs_2_) | copy-start | bytes 3342340
  166.5 54.5 %collective-permute-start.6 = (bf16[1056,128]{1,0:T(8,128)(2,1)}, bf16[1056,128]{1,0:T(8,128)(2,1)S(1)}, u32[]{:S(2)}, u32[]{:S(2)}) collective-permute-start(bf16[1056,128]{1,0:T(8,128)(2,1)} %get-tuple-element.42), channel_id=1, source_target_pairs={{0,14},{2,12},{4,10},{6,8},{8,6},{10,4},{12,2},{14,0},{1,15},{3,13... | collective-permute-start | bytes 811016 | tf_op jit(solution)/shard_map/ppermute | solution.py:703
  189.8 1.0 copy-start.2
  197.9 39.4 %collective-permute-start.10 = (bf16[1056,128]{1,0:T(8,128)(2,1)}, bf16[1056,128]{1,0:T(8,128)(2,1)S(1)}, u32[]{:S(2)}, u32[]{:S(2)}) collective-permute-start(bf16[1056,128]{1,0:T(8,128)(2,1)} %get-tuple-element.51), channel_id=1, source_target_pairs={{0,8},{2,10},{4,12},{6,14},{8,0},{10,2},{12,4},{14,6},{1,9},{3,11}... | collective-permute-start | bytes 811016 | tf_op jit(solution)/shard_map/ppermute | solution.py:703
  198.0 0.7 copy-start.4
  198.0 0.9 copy-start.5
  213.4 30.7 %collective-permute-start.11 = (bf16[1056,128]{1,0:T(8,128)(2,1)}, bf16[1056,128]{1,0:T(8,128)(2,1)S(1)}, u32[]{:S(2)}, u32[]{:S(2)}) collective-permute-start(bf16[1056,128]{1,0:T(8,128)(2,1)} %get-tuple-element.52), channel_id=1, source_target_pairs={{0,10},{2,8},{4,14},{6,12},{8,2},{10,0},{12,6},{14,4},{1,11},{3,9}... | collective-permute-start | bytes 811016 | tf_op jit(solution)/shard_map/ppermute | solution.py:703
  216.3 43.1 %collective-permute-start.15 = (bf16[1056,128]{1,0:T(8,128)(2,1)}, bf16[1056,128]{1,0:T(8,128)(2,1)S(1)}, u32[]{:S(2)}, u32[]{:S(2)}) collective-permute-start(bf16[1056,128]{1,0:T(8,128)(2,1)} %get-tuple-element.60), channel_id=1, source_target_pairs={{0,12},{2,14},{4,8},{6,10},{8,4},{10,6},{12,0},{14,2},{1,13},{3,15... | collective-permute-start | bytes 811016 | tf_op jit(solution)/shard_map/ppermute | solution.py:703
  218.4 2.7 copy-start.9
  218.4 63.4 %collective-permute-start.16 = (bf16[1056,128]{1,0:T(8,128)(2,1)}, bf16[1056,128]{1,0:T(8,128)(2,1)S(1)}, u32[]{:S(2)}, u32[]{:S(2)}) collective-permute-start(bf16[1056,128]{1,0:T(8,128)(2,1)} %get-tuple-element.61), channel_id=1, source_target_pairs={{0,14},{2,12},{4,10},{6,8},{8,6},{10,4},{12,2},{14,0},{1,15},{3,13... | collective-permute-start | bytes 811016 | tf_op jit(solution)/shard_map/ppermute | solution.py:703
  221.0 0.7 copy-start.10
  233.9 26.2 %collective-permute-start.12 = (bf16[1056,128]{1,0:T(8,128)(2,1)}, bf16[1056,128]{1,0:T(8,128)(2,1)S(1)}, u32[]{:S(2)}, u32[]{:S(2)}) collective-permute-start(bf16[1056,128]{1,0:T(8,128)(2,1)} %get-tuple-element.55), channel_id=1, source_target_pairs={{0,2},{2,0},{4,6},{6,4},{8,10},{10,8},{12,14},{14,12},{1,3},{3,1},... | collective-permute-start | bytes 811016 | tf_op jit(solution)/shard_map/ppermute | solution.py:703
  237.3 6.8 %copy-start.6 = (bf16[1056,128]{1,0:T(8,128)(2,1)}, bf16[1056,128]{1,0:T(8,128)(2,1)S(1)}, u32[]{:S(2)}) copy-start(bf16[1056,128]{1,0:T(8,128)(2,1)S(1)} %collective-permute-done.10.refs_10_.refs_0_.refs_9_) | copy-start | bytes 811012
  237.3 25.0 %collective-permute-start.13 = (bf16[1056,128]{1,0:T(8,128)(2,1)}, bf16[1056,128]{1,0:T(8,128)(2,1)S(1)}, u32[]{:S(2)}, u32[]{:S(2)}) collective-permute-start(bf16[1056,128]{1,0:T(8,128)(2,1)} %get-tuple-element.56), channel_id=1, source_target_pairs={{0,4},{2,6},{4,0},{6,2},{8,12},{10,14},{12,8},{14,10},{1,5},{3,7},... | collective-permute-start | bytes 811016 | tf_op jit(solution)/shard_map/ppermute | solution.py:703
  244.1 0.7 copy-start.7
  244.1 31.8 %collective-permute-start.14 = (bf16[1056,128]{1,0:T(8,128)(2,1)}, bf16[1056,128]{1,0:T(8,128)(2,1)S(1)}, u32[]{:S(2)}, u32[]{:S(2)}) collective-permute-start(bf16[1056,128]{1,0:T(8,128)(2,1)} %get-tuple-element.57), channel_id=1, source_target_pairs={{0,6},{2,4},{4,2},{6,0},{8,14},{10,12},{12,10},{14,8},{1,7},{3,5},... | collective-permute-start | bytes 811016 | tf_op jit(solution)/shard_map/ppermute | solution.py:703
  259.5 9.3 %copy-start.8 = (bf16[1056,128]{1,0:T(8,128)(2,1)}, bf16[1056,128]{1,0:T(8,128)(2,1)S(1)}, u32[]{:S(2)}) copy-start(bf16[1056,128]{1,0:T(8,128)(2,1)S(1)} %collective-permute-done.15.refs_19_.refs_2_.refs_11_) | copy-start | bytes 811012
  259.5 22.3 %collective-permute-start.17 = (bf16[1056,128]{1,0:T(8,128)(2,1)}, bf16[1056,128]{1,0:T(8,128)(2,1)S(1)}, u32[]{:S(2)}, u32[]{:S(2)}) collective-permute-start(bf16[1056,128]{1,0:T(8,128)(2,1)} %get-tuple-element.63), channel_id=1, source_target_pairs={{0,2},{2,0},{4,6},{6,4},{8,10},{10,8},{12,14},{14,12},{1,3},{3,1},... | collective-permute-start | bytes 811016 | tf_op jit(solution)/shard_map/ppermute | solution.py:703
  260.1 8.7 %copy-start.12 = (bf16[1056,128]{1,0:T(8,128)(2,1)}, bf16[1056,128]{1,0:T(8,128)(2,1)S(1)}, u32[]{:S(2)}) copy-start(bf16[1056,128]{1,0:T(8,128)(2,1)S(1)} %collective-permute-done.12.refs_5_.refs_14_) | copy-start | bytes 811012
  260.1 21.7 %collective-permute-start.18 = (bf16[1056,128]{1,0:T(8,128)(2,1)}, bf16[1056,128]{1,0:T(8,128)(2,1)S(1)}, u32[]{:S(2)}, u32[]{:S(2)}) collective-permute-start(bf16[1056,128]{1,0:T(8,128)(2,1)} %get-tuple-element.64), channel_id=1, source_target_pairs={{0,4},{2,6},{4,0},{6,2},{8,12},{10,14},{12,8},{14,10},{1,5},{3,7},... | collective-permute-start | bytes 811016 | tf_op jit(solution)/shard_map/ppermute | solution.py:703
  262.3 6.5 %copy-start.14 = (bf16[1056,128]{1,0:T(8,128)(2,1)}, bf16[1056,128]{1,0:T(8,128)(2,1)S(1)}, u32[]{:S(2)}) copy-start(bf16[1056,128]{1,0:T(8,128)(2,1)S(1)} %collective-permute-done.13.refs_6_.refs_15_) | copy-start | bytes 811012
  262.3 19.5 %collective-permute-start.19 = (bf16[1056,128]{1,0:T(8,128)(2,1)}, bf16[1056,128]{1,0:T(8,128)(2,1)S(1)}, u32[]{:S(2)}, u32[]{:S(2)}) collective-permute-start(bf16[1056,128]{1,0:T(8,128)(2,1)} %get-tuple-element.65), channel_id=1, source_target_pairs={{0,6},{2,4},{4,2},{6,0},{8,14},{10,12},{12,10},{14,8},{1,7},{3,5},... | collective-permute-start | bytes 811016 | tf_op jit(solution)/shard_map/ppermute | solution.py:703
  275.9 0.7 copy-start.16
  281.8 0.7 copy-start.11
  281.8 0.8 copy-start.13
  281.8 0.9 copy-start.15
  281.9 0.9 copy-start.17
